TPU v7x, 128 devices: a whole 4x4x4 slice. The times are simulated.
128 devices in a mesh: dp: 8 (over z_lo, y), ctx: 16 (over z_hi, x, core).
Axes of the slice: x: 4, y: 4, z: 4 (z_hi: 2, z_lo: 2; z = z_hi * 2 + z_lo), core: 2. Of those that a mesh axis runs over, the one named last changes fastest.
Arguments:
- tokens: bfloat16 [16, 1024, 1536], P('dp', 'ctx'), may hold values from -6 to 6
- doc_start: int32 [16, 1024], P('dp'), may hold values from 0 to 1, as said below
- gain_attn: bfloat16 [1536], P(('dp', 'ctx')), may hold values from 0.5 to 1.5
- w_query: bfloat16 [1536, 1536], P(('dp', 'ctx')), may hold values from -0.15625 to 0.15625
- w_key: bfloat16 [1536, 1536], P(('dp', 'ctx')), may hold values from -0.15625 to 0.15625
- w_value: bfloat16 [1536, 1536], P(('dp', 'ctx')), may hold values from -0.15625 to 0.15625
- w_path: bfloat16 [1536, 1536], P(('dp', 'ctx')), may hold values from -0.15625 to 0.15625
- conv_path: bfloat16 [4, 1536], P(None, ('dp', 'ctx')), may hold values from -3 to 3
- w_beta: bfloat16 [1536, 12], P(('dp', 'ctx')), may hold values from -0.15625 to 0.15625
- w_out: bfloat16 [1536, 1536], P(('dp', 'ctx')), may hold values from -0.625 to 0.625
- gain_ffn: bfloat16 [1536], P(('dp', 'ctx')), may hold values from 0.5 to 1.5
- w_gate: bfloat16 [1536, 4096], P(('dp', 'ctx')), may hold values from -0.15625 to 0.15625
- w_up: bfloat16 [1536, 4096], P(('dp', 'ctx')), may hold values from -0.15625 to 0.15625
- w_down: bfloat16 [4096, 1536], P(('dp', 'ctx')), may hold values from -0.09375 to 0.09375
- grad_out: bfloat16 [16, 1024, 1536], P('dp', 'ctx'), may hold values from -6 to 6
Outputs:
- output: bfloat16 [16, 1024, 1536], P('dp', 'ctx')
- d_tokens: bfloat16 [16, 1024, 1536], P('dp', 'ctx')
- d_gain_attn: float32 [1536], P(('dp', 'ctx'))
- d_w_query: float32 [1536, 1536], P(('dp', 'ctx'))
- d_w_key: float32 [1536, 1536], P(('dp', 'ctx'))
- d_w_value: float32 [1536, 1536], P(('dp', 'ctx'))
- d_w_path: float32 [1536, 1536], P(('dp', 'ctx'))
- d_conv_path: float32 [4, 1536], P(None, ('dp', 'ctx'))
- d_w_beta: float32 [1536, 12], P(('dp', 'ctx'))
- d_w_out: float32 [1536, 1536], P(('dp', 'ctx'))
- d_gain_ffn: float32 [1536], P(('dp', 'ctx'))
- d_w_gate: float32 [1536, 4096], P(('dp', 'ctx'))
- d_w_up: float32 [1536, 4096], P(('dp', 'ctx'))
- d_w_down: float32 [4096, 1536], P(('dp', 'ctx'))
Inputs may be any that keep to these rules, and one draw needn't show every extreme that they name: `doc_start`: position 0 of every row is 1. Of the 2 rows held by each index of dp, one has a document that begins within the first 64 positions and ends within the last 64.
All inputs are finite; a program needn't handle non-finite values.
Results may differ from a plain program's by a relative error of at most 0.025.
Values may be sent and summed in bfloat16 or wider, within the bound.
A program may use at most 384 MiB of HBM per device.

v0:
```python
import functools

import jax
import jax.numpy as jnp
from jax import lax
from jax.experimental import pallas as pl
from jax.experimental.pallas import tpu as pltpu
from jax.sharding import Mesh, PartitionSpec as P

F32, BF16 = jnp.float32, jnp.bfloat16
VM = 61 * 1024 * 1024

SEQ, HD, BLK = 1024, 128, 128
NB = SEQ // BLK
NQC = (NB * (NB - 1) // 2) * BLK
SCALE = HD ** (-0.5)
GROUP, GROUP_BACK = 8, 4


def mm(a, b, dims=((1,), (0,))):
    return lax.dot_general(
        a.astype(BF16), b.astype(BF16), (dims, ((), ())), preferred_element_type=F32
    )


def mm_nt(a, b):
    return mm(a, b, ((1,), (1,)))


def mm_tn(a, b):
    return mm(a, b, ((0,), (0,)))


def split(a):
    high = a.astype(BF16)
    return high, (a - high.astype(F32)).astype(BF16)


def mm3(a, b):
    ah, al = split(a)
    bh, bl = split(b)
    return mm(ah, bh) + (mm(ah, bl) + mm(al, bh))


def iota2(axis):
    return lax.broadcasted_iota(jnp.int32, (BLK, BLK), axis)


BASE = 16


def unit_inverses(lowers):
    row, col = iota2(0), iota2(1)
    eye = (row == col).astype(F32)
    in_base = (row // BASE) == (col // BASE)
    narrow = [jnp.where(in_base, low, 0.0) for low in lowers]
    inv = [eye for _ in lowers]
    for u in range(BASE - 1):
        pick = (col % BASE) == u
        coef = [jnp.sum(jnp.where(pick, low, 0.0), axis=1, keepdims=True) for low in narrow]
        for n, (t, c) in enumerate(zip(inv, coef)):
            t3 = t.reshape(BLK // BASE, BASE, BLK)
            lead = jnp.broadcast_to(t3[:, u : u + 1, :], t3.shape).reshape(BLK, BLK)
            inv[n] = t - c * lead
    size = BASE
    while size < BLK:
        off = ((row // (2 * size)) == (col // (2 * size))) & ((row // size) != (col // size))
        mid = [mm3(t, jnp.where(off, low, 0.0)) for t, low in zip(inv, lowers)]
        inv = [t - mm3(m, t) for t, m in zip(inv, mid)]
        size *= 2
    return inv


def betas_of(raw, head):
    lane = lax.broadcasted_iota(jnp.int32, raw.shape, 1)
    return 2.0 * jax.nn.sigmoid(
        jnp.sum(jnp.where(lane == head + BETA_AT, raw, 0.0), axis=1, keepdims=True)
    )


BETA_AT = 6
CONV_AT = 2
TAPS = 4


def conv_weights(small, head):
    part = small[pl.ds(pl.multiple_of(head * HD, HD), HD), :].astype(F32)
    return part.T[CONV_AT : CONV_AT + TAPS, :]


def convolve(path, taps, marks):
    total = taps[0:1, :] * path
    for m in range(1, TAPS):
        total = total + taps[m : m + 1, :] * (pltpu.roll(path, m, 0) * marks[:, m : m + 1])
    return total


def own_blocks(s, q, k, w, bcol, stores):
    t_out, a_out, z_out, m_out, kp_out, qm_buf, s_buf = stores
    row, col = iota2(0), iota2(1)
    strict, closed = row > col, row >= col
    eye = (row == col).astype(F32)

    def group(g, carry):
        sl = [pl.ds(pl.multiple_of((g * GROUP + n) * BLK, BLK), BLK) for n in range(GROUP)]
        qs = [q[r, :] for r in sl]
        ks = [k[r, :] for r in sl]
        ws = [w[r, :] for r in sl]
        bc = [jnp.broadcast_to(bcol[r, :], (BLK, BLK)) for r in sl]
        br = [b.T for b in bc]
        low = [jnp.where(strict, mm_nt(x, x), 0.0) * b for x, b in zip(ws, br)]
        inv = unit_inverses(low)
        m1 = [jnp.where(strict, mm_nt(x, y), 0.0) for x, y in zip(ws, ks)]
        gq = [jnp.where(closed, mm_nt(x, y), 0.0) * b for x, y, b in zip(qs, ws, br)]
        a = [mm(x, t) for x, t in zip(gq, inv)]
        z = [mm_tn(t, b * x.astype(F32)) for t, b, x in zip(inv, bc, ws)]
        sd = [mm_nt(x, y) - mm(p, m) for x, y, p, m in zip(qs, ks, a, m1)]
        qm = [x.astype(F32) - mm(p, y) for x, p, y in zip(qs, a, ws)]
        kmt = [x.astype(F32).T - mm_tn(zz, m) for x, zz, m in zip(ks, z, m1)]
        pm = [eye - mm_tn(zz, x) for zz, x in zip(z, ws)]
        for n, r in enumerate(sl):
            t_out[s, r, :] = inv[n].astype(t_out.dtype)
            a_out[s, r, :] = a[n].astype(a_out.dtype)
            z_out[s, r, :] = z[n].astype(z_out.dtype)
            m_out[s, r, :] = m1[n].astype(m_out.dtype)
            kp_out[s, r, :HD] = kmt[n].astype(BF16)
            kp_out[s, r, HD:] = pm[n].astype(BF16)
            qm_buf[r, :] = qm[n]
            s_buf[r, r] = sd[n]
        return carry

    lax.fori_loop(0, NB // GROUP, group, 0)


def sweep(s, qc, kp, qm_buf, x_buf, s_buf):
    at = NQC
    for j in range(NB - 2, -1, -1):
        r0 = (j + 1) * BLK
        rows = SEQ - r0
        x_buf[r0 : r0 + BLK, :] = qm_buf[r0 : r0 + BLK, :]
        x = x_buf[r0:, :].astype(BF16)
        at -= rows
        qc[s, at : at + rows, :] = x
        both = mm(x, kp[s, j * BLK : r0, :])
        s_buf[r0:, j * BLK : r0] = both[:, :HD]
        x_buf[r0:, :] = both[:, HD:]


def weigh(s, v, dcol, drow, s_buf, probs, o):
    for i in range(NB):
        lo, width = i * BLK, (i + 1) * BLK
        t = s_buf[lo:width, :width] * SCALE
        seen = dcol[lo:width, 0:1] == drow[0:1, :width]
        seen = seen & (
            lax.broadcasted_iota(jnp.int32, (BLK, width), 0) + lo
            >= lax.broadcasted_iota(jnp.int32, (BLK, width), 1)
        )
        t = jnp.where(seen, t, -1e30)
        e = jnp.exp(t - jnp.max(t, axis=1, keepdims=True))
        p = (e * (1.0 / jnp.sum(e, axis=1, keepdims=True))).astype(BF16)
        probs[s, lo:width, :width] = p
        o[lo:width, :] = mm(p, v[:width, :])


def project(x_all, whole, gains, normed, qkvp, raw):
    rows = 256
    width = x_all.shape[1]
    for n in range(width // HD):
        cols = slice(n * HD, (n + 1) * HD)
        gains[:, cols] = whole[cols, 8 * HD : 9 * HD].astype(F32).T[:8, :]

    def block(i, carry):
        at = pl.ds(pl.multiple_of(i * rows, rows), rows)
        x = x_all[at, :].astype(F32)
        scale = lax.rsqrt(jnp.mean(x * x, axis=1, keepdims=True) + 1e-05)
        n = (x * scale * gains[0:1, :]).astype(BF16)
        normed[at, :] = n
        y = mm(n, whole[:, : 9 * HD])
        qkvp[at, :] = y[:, : 8 * HD].astype(BF16)
        raw[at, :] = y[:, 8 * HD :]
        return carry

    lax.fori_loop(0, SEQ // rows, block, 0)


def heads_here():
    chip, core = lax.axis_index("x"), lax.axis_index("c")
    return 3 * chip + 2 * core, 3 * chip + 1


def fwd_slot(poke, s, head, small, marks, drow, qkvp, raw, vec, o, probs, qc, t_out, a_out, z_out, m_out, kp_out, s_buf, x_buf, qm_buf, b_buf):
    cols = slice(s * HD, (s + 1) * HD)
    q, k, v, path = (qkvp.at[:, (4 * s + n) * HD : (4 * s + n + 1) * HD] for n in range(4))
    taps = conv_weights(small, head)
    conved = convolve(path[...].astype(F32), taps, marks[...])
    unit = conved * lax.rsqrt(jnp.sum(conved * conved, axis=1, keepdims=True) + 1e-06)
    vec[:, cols] = unit.astype(BF16)
    b_buf[...] = betas_of(raw[...], head)
    own_blocks(s, q, k, vec.at[:, cols], b_buf, (t_out, a_out, z_out, m_out, kp_out, qm_buf, s_buf))
    poke()
    sweep(s, qc, kp_out, qm_buf, x_buf, s_buf)
    poke()
    weigh(s, v, marks, drow, s_buf, probs, o.at[:, cols])


def score_grads(s, v, o, do, probs, ds_buf, dv):
    for i in range(NB):
        lo, width = i * BLK, (i + 1) * BLK
        p = probs[0, lo:width, :width].astype(F32)
        g = do[lo:width, :]
        delta = jnp.sum(g * o[lo:width, :].astype(F32), axis=1, keepdims=True)
        ds = p * (mm_nt(g, v[:width, :]) - delta) * SCALE
        ds_buf[lo:width, :width] = ds.astype(BF16)
    for j in range(NB):
        lo = j * BLK
        dv[lo : lo + BLK, :] = mm_tn(probs[0, lo:, lo : lo + BLK], do[lo:, :]).astype(dv.dtype)


def sweep_back(s, qc, kp, ds_buf, x_buf, dkm_buf, dpm_buf):
    x_buf[...] = jnp.zeros_like(x_buf)
    dkm_buf[SEQ - BLK :, :] = jnp.zeros((BLK, HD), F32)
    dpm_buf[SEQ - BLK :, :] = jnp.zeros((BLK, HD), F32)
    at = 0
    for j in range(NB - 1):
        lo, r0 = j * BLK, (j + 1) * BLK
        rows = SEQ - r0
        x = x_buf[r0:, :].astype(BF16)
        ds = ds_buf[r0:, lo:r0]
        qcj = qc[0, at : at + rows, :]
        at += rows
        both = mm_tn(qcj, jnp.concatenate([x, ds], axis=1))
        dpm_buf[lo:r0, :] = both[:, :HD]
        dkm_buf[lo:r0, :] = both[:, HD:].T
        x_buf[r0:, :] = mm_nt(jnp.concatenate([ds, x], axis=1), kp[0, lo:r0, :])


def own_blocks_back(s, q, k, w, bcol, saved, bufs, dq, dk, dw, db):
    t_in, a_in, z_in, m_in = saved
    ds_buf, x_buf, dkm_buf, dpm_buf = bufs
    row, col = iota2(0), iota2(1)
    strict, closed = row > col, row >= col

    def group(g, carry):
        sl = [pl.ds(pl.multiple_of((g * GROUP_BACK + n) * BLK, BLK), BLK) for n in range(GROUP_BACK)]
        rng = range(GROUP_BACK)
        Q = [q[r, :] for r in sl]
        K = [k[r, :] for r in sl]
        W = [w[r, :] for r in sl]
        bc = [jnp.broadcast_to(bcol[r, :], (BLK, BLK)) for r in sl]
        br = [b.T for b in bc]
        E = [ds_buf[r, r] for r in sl]
        T = [t_in[0, r, :] for r in sl]
        A = [a_in[0, r, :] for r in sl]
        Z = [z_in[0, r, :] for r in sl]
        M = [m_in[0, r, :] for r in sl]
        dQm = [x_buf[r, :] for r in sl]
        dKm = [dkm_buf[r, :] for r in sl]
        dPm = [dpm_buf[r, :] for r in sl]
        i1 = [mm_nt(W[n], W[n]) for n in rng]
        qw = [jnp.where(closed, mm_nt(Q[n], W[n]), 0.0) for n in rng]
        dA = [-(mm_nt(E[n], M[n]) + mm_nt(dQm[n], W[n])) for n in rng]
        dM = [jnp.where(strict, -(mm_tn(A[n], E[n]) + mm_nt(Z[n], dKm[n])), 0.0) for n in rng]
        dZ = [-(mm(M[n], dKm[n]) + mm_nt(W[n], dPm[n])) for n in rng]
        dW = [-(mm_tn(A[n], dQm[n]) + mm(Z[n], dPm[n])) for n in rng]
        dG = [jnp.where(closed, mm_nt(dA[n], T[n]), 0.0) for n in rng]
        bw = [bc[n] * W[n].astype(F32) for n in rng]
        dT = [mm_tn(qw[n] * br[n], dA[n]) + mm_nt(bw[n], dZ[n]) for n in rng]
        dBW = [mm(T[n], dZ[n]) for n in rng]
        dL = [mm_tn(T[n], dT[n]) for n in rng]
        dL = [jnp.where(strict, -mm_nt(dL[n], T[n]), 0.0) for n in rng]
        dI = [dL[n] * br[n] for n in rng]
        R = [dG[n] * br[n] for n in rng]
        for n, r in enumerate(sl):
            db[r, :] = jnp.sum(
                (dL[n] * i1[n] + dG[n] * qw[n]).T + dBW[n] * W[n].astype(F32), axis=1, keepdims=True
            )
            dq[r, :] = (dQm[n] + mm(E[n], K[n]) + mm(R[n], W[n])).astype(dq.dtype)
            dk[r, :] = (dKm[n] + mm_tn(E[n], Q[n]) + mm_tn(dM[n], W[n])).astype(dk.dtype)
            dw[r, :] = (
                dW[n]
                + bc[n] * dBW[n]
                + mm_tn(R[n], Q[n])
                + mm(dM[n], K[n])
                + mm(dI[n] + dI[n].T, W[n])
            )
        return carry

    lax.fori_loop(0, NB // GROUP_BACK, group, 0)


def bwd_slot(poke, s, head, qkvp, raw, small, marks, vec, o, do, probs, qc, t_in, a_in, z_in, m_in, kp, d_ext, d_conv, ds_buf, x_buf, dkm_buf, dpm_buf, b_buf, db_buf, dw_buf):
    cols = slice(s * HD, (s + 1) * HD)
    q, k, v, path = (qkvp.at[:, (4 * s + n) * HD : (4 * s + n + 1) * HD] for n in range(4))
    dq, dk, dv, dpath = (d_ext.at[:, (4 * s + n) * HD : (4 * s + n + 1) * HD] for n in range(4))
    score_grads(s, v, o.at[:, cols], do.at[:, cols], probs, ds_buf, dv)
    poke()
    sweep_back(s, qc, kp, ds_buf, x_buf, dkm_buf, dpm_buf)
    poke()
    beta = betas_of(raw[...], head)
    b_buf[...] = beta
    own_blocks_back(
        s, q, k, vec.at[:, cols], b_buf, (t_in, a_in, z_in, m_in), (ds_buf, x_buf, dkm_buf, dpm_buf), dq, dk, dw_buf, db_buf
    )
    poke()
    taps = conv_weights(small, head)
    raw_path = path[...].astype(F32)
    conved = convolve(raw_path, taps, marks[...])
    scale = lax.rsqrt(jnp.sum(conved * conved, axis=1, keepdims=True) + 1e-06)
    unit = conved * scale
    dw = dw_buf[...]
    d_conved = scale * (dw - unit * jnp.sum(dw * unit, axis=1, keepdims=True))
    total = taps[0:1, :] * d_conved
    d_conv[s, 0:1, :] = jnp.sum(d_conved * raw_path, axis=0, keepdims=True)
    for m in range(1, TAPS):
        marked = d_conved * marks[:, m : m + 1]
        d_conv[s, m : m + 1, :] = jnp.sum(marked * pltpu.roll(raw_path, m, 0), axis=0, keepdims=True)
        total = total + taps[m : m + 1, :] * pltpu.roll(marked, SEQ - m, 0)
    dpath[...] = total.astype(dpath.dtype)
    lane = lax.broadcasted_iota(jnp.int32, (SEQ, HD), 1)
    return jnp.where(lane == head + BETA_AT, db_buf[...] * beta * (1.0 - 0.5 * beta), 0.0)


def fwd_shapes(width):
    return [
        ((SEQ, width), BF16),
        ((SEQ, 8 * HD), BF16),
        ((SEQ, HD), F32),
        ((SEQ, 2 * HD), BF16),
        ((SEQ, 2 * HD), BF16),
        ((8, width), F32),
        ((2, SEQ, SEQ), BF16),
        ((2, NQC, HD), BF16),
        ((2, SEQ, BLK), BF16),
        ((2, SEQ, BLK), BF16),
        ((2, SEQ, BLK), BF16),
        ((2, SEQ, BLK), BF16),
        ((2, SEQ, 2 * HD), BF16),
    ]


def fwd_scratch():
    return [
        pltpu.VMEM((SEQ, SEQ), F32),
        pltpu.VMEM((SEQ, HD), F32),
        pltpu.VMEM((SEQ, HD), F32),
        pltpu.VMEM((SEQ, 1), F32),
    ]


def bwd_scratch():
    return (
        [pltpu.VMEM((SEQ, SEQ), BF16)]
        + [pltpu.VMEM((SEQ, HD), F32)] * 3
        + [pltpu.VMEM((SEQ, 1), F32)] * 2
        + [pltpu.VMEM((SEQ, HD), F32)]
    )


MESH = pl.DeviceIdType.MESH
ANY = pl.BlockSpec(memory_space=pl.ANY)
VMEM = pl.BlockSpec(memory_space=pltpu.VMEM)


class Place:
    def __init__(self):
        self.x, self.c = lax.axis_index("x"), lax.axis_index("c")
        self.y = lax.axis_index("y")
        self.zl, self.zh = lax.axis_index("zl"), lax.axis_index("zh")
        self.z = self.zh * 2 + self.zl

    def chip(self, d):
        return lax.rem(self.x + d, 4)

    def at_x(self, d):
        return {"x": lax.rem(self.x + d, 4)}

    def at_xc(self, d, k):
        return {"x": lax.rem(self.x + d, 4), "c": lax.rem(self.c + k, 2)}

    def sibling(self):
        return {"c": 1 - self.c}

    def at_y(self, d):
        return {"y": lax.rem(self.y + d, 4)}

    def at_z(self, d):
        z = lax.rem(self.z + d, 4)
        return {"zl": lax.rem(z, 2), "zh": z // 2}


class Net:
    def __init__(self, send_sem, recv_sem, local_sem):
        self.place = Place()
        self.send_sem, self.recv_sem, self.local_sem = send_sem, recv_sem, local_sem
        self.count, self.kept, self.locals, self.sent = 0, 0, [], []

    def prepare(self, src, dst, device):
        k = self.count
        self.count += 1
        return pltpu.make_async_remote_copy(
            src_ref=src,
            dst_ref=dst,
            send_sem=self.send_sem.at[k],
            recv_sem=self.recv_sem.at[k],
            device_id=device,
            device_id_type=MESH,
        )

    def send(self, src, dst, device):
        copy = self.prepare(src, dst, device)
        copy.start()
        self.sent.append(copy)
        return copy

    def local(self, src, dst):
        self.kept += 1
        return pltpu.make_async_copy(src, dst, self.local_sem.at[self.kept - 1])

    def load(self, src, dst):
        copy = self.local(src, dst)
        copy.start()
        return copy

    def keep(self, src, dst):
        self.locals.append(self.load(src, dst))

    def settle(self):
        for copy in self.locals:
            copy.wait()
        self.locals = []

    def finish(self):
        for copy in self.sent:
            copy.wait_send()
        self.settle()


def meet(devices):
    barrier = pltpu.get_barrier_semaphore()
    for device in devices:
        pl.semaphore_signal(barrier, inc=1, device_id=device, device_id_type=MESH)
    pl.semaphore_wait(barrier, len(devices))


class Jobs:
    def __init__(self, *jobs):
        self.all = list(jobs)
        self.jobs = list(jobs)

    def poke(self):
        for job in list(self.jobs):
            try:
                next(job)
            except StopIteration:
                self.jobs.remove(job)

    def step(self, *which):
        for n in which:
            next(self.all[n], None)

    def drain(self):
        while self.jobs:
            self.poke()


def interleave(*jobs):
    Jobs(*jobs).drain()


def team_peers(p):
    return [p.at_x(1), p.at_x(3), p.sibling()]


def team_all(p):
    return [p.at_xc(d, k) for d in range(4) for k in range(2) if d + k]


def group_peers(p):
    return [p.at_y(d) for d in (1, 2, 3)] + [p.at_z(d) for d in (1, 2, 3)]


def gather_team(net, own, out):
    p = net.place
    me, sib = 2 * p.x + p.c, p.sibling()
    right, left = p.at_x(1), p.at_x(3)
    t_l, t_r, t_2 = (2 * p.chip(d) + p.c for d in (3, 1, 2))
    to_r = net.send(own, out.at[:, me], right)
    to_l = net.send(own, out.at[:, me], left)
    shared = [net.send(own, out.at[:, me], sib)]
    net.keep(own, out.at[:, me])
    yield
    to_r.wait_recv()
    on_r = net.send(out.at[0, t_l], out.at[0, t_l], right)
    shared.append(net.send(out.at[:, t_l], out.at[:, t_l], sib))
    to_l.wait_recv()
    on_l = net.send(out.at[1, t_r], out.at[1, t_r], left)
    shared.append(net.send(out.at[:, t_r], out.at[:, t_r], sib))
    yield
    on_r.wait_recv()
    shared.append(net.send(out.at[0, t_2], out.at[0, t_2], sib))
    on_l.wait_recv()
    shared.append(net.send(out.at[1, t_2], out.at[1, t_2], sib))
    yield
    for copy in shared:
        copy.wait_recv()


GATHER_TEAM = 10


def add(a, b):
    return (a.astype(F32) + b.astype(F32)).astype(BF16)


def scatter_team(net, part, got, total, from_l, from_r, all_l, all_r, finish):
    p = net.place
    sib, right, left = p.sibling(), p.at_x(1), p.at_x(3)
    order = (2, 1, 3, 0)
    swaps, loads = [], []
    for d in order:
        at = p.chip(d)
        swaps.append(net.send(part.at[:, 2 * at + 1 - p.c], got.at[:, at], sib))
        loads.append(net.load(part.at[:, 2 * at + p.c], total.at[:, at]))

    def pair(n):
        swaps[n].wait_recv()
        loads[n].wait()
        at = p.chip(order[n])
        total[:, at] = add(total[:, at], got[:, at])
        return at

    yield
    x_2 = pair(0)
    half_r = net.send(total.at[0, x_2], from_l, right)
    half_l = net.send(total.at[1, x_2], from_r, left)
    x_r = pair(1)
    rest_r = net.send(total.at[1, x_r], all_l.at[1], right)
    x_l = pair(2)
    rest_l = net.send(total.at[0, x_l], all_r.at[0], left)
    pair(3)
    yield
    half_r.wait_recv()
    total[0, x_r] = add(total[0, x_r], from_l[...])
    last_r = net.send(total.at[0, x_r], all_l.at[0], right)
    half_l.wait_recv()
    total[1, x_l] = add(total[1, x_l], from_r[...])
    last_l = net.send(total.at[1, x_l], all_r.at[1], left)
    yield
    for copy in (rest_r, rest_l, last_r, last_l):
        copy.wait_recv()
    finish(total[:, p.x].astype(F32) + all_l[...].astype(F32) + all_r[...].astype(F32))


SCATTER_TEAM_LOADS = 4
SCATTER_TEAM = 10


def scatter_team_scratch(n, w):
    return [
        pltpu.VMEM((2, 4, n, w), BF16),
        pltpu.VMEM((2, 4, n, w), BF16),
        pltpu.VMEM((n, w), BF16),
        pltpu.VMEM((n, w), BF16),
        pltpu.VMEM((2, n, w), BF16),
        pltpu.VMEM((2, n, w), BF16),
    ]


def chunk_rows(y, z, rows):
    zl, zh = (z % 2, z // 2) if isinstance(z, int) else (lax.rem(z, 2), z // 2)
    return pl.ds(pl.multiple_of(((zl * 4 + y) * 2 + zh) * rows, rows), rows)


def halves(cols):
    mid = cols // 2
    return [(pl.ds(0, mid),) * 2], [(pl.ds(mid, cols - mid),) * 2]


def gather_groups(net, own, out, y_pieces, z_pieces, share=False):
    p = net.place
    rows = own.shape[0]
    shared = []
    for src, dst in y_pieces + z_pieces:
        net.keep(own.at[:, src], out.at[chunk_rows(p.y, p.z, rows), dst])

    def spread(pieces, y, z, devices, first=False):
        copies = []
        for src, dst in pieces:
            place = out.at[chunk_rows(y, z, rows), dst]
            copies += [net.send(own.at[:, src] if first else place, place, d) for d in devices]
        return copies

    def give(y, z, first=False):
        if share:
            src, dst = z_pieces[-1]
            place = out.at[chunk_rows(y, z, rows), dst]
            shared.append(net.send(own.at[:, src] if first else place, place, p.sibling()))

    order = (1, 3, 2)
    ys, zs = [p.at_y(d) for d in order], [p.at_z(d) for d in order]
    y_first = spread(y_pieces, p.y, p.z, ys, True)
    z_first = spread(z_pieces, p.y, p.z, zs, True)
    last = spread(y_pieces, p.y, p.z, zs, True)
    via_y = [(p.z, spread(z_pieces, p.y, p.z, ys, True))]
    give(p.y, p.z, True)
    yield
    for n, d in enumerate(order):
        for copy in y_first[n::3]:
            copy.wait_recv()
        last += spread(y_pieces, lax.rem(p.y + 4 - d, 4), p.z, zs)
        for copy in z_first[n::3]:
            copy.wait_recv()
        z = lax.rem(p.z + 4 - d, 4)
        via_y.append((z, spread(z_pieces, p.y, z, ys)))
        give(p.y, z)
        yield
    for z, copies in via_y:
        for n, d in enumerate(order):
            for copy in copies[n::3]:
                copy.wait_recv()
            give(lax.rem(p.y + 4 - d, 4), z)
    for copy in last + shared:
        copy.wait_recv()


GATHER_GROUPS = 30


def scatter_groups(net, part, out, cuts, z_got, z_sum, z_last, y_got, y_sum, y_last):
    p = net.place
    lo, mid, hi = cuts
    first, second = pl.ds(lo, mid - lo), pl.ds(mid, hi - mid)
    rows = z_sum.shape[1]
    both = hi > mid
    flat = len(part.shape) == 2
    order = (2, 1, 3)
    a, b, a_own, b_own = [], [], [], []
    for n, d in enumerate(order):
        z, y = lax.rem(p.z + d, 4), lax.rem(p.y + d, 4)
        if flat:
            for k in range(4):
                a.append(net.send(part.at[chunk_rows(k, z, rows), first], z_got.at[n, k], p.at_z(d)))
                if both:
                    b.append(net.send(part.at[chunk_rows(y, k, rows), second], y_got.at[n, k % 2, k // 2], p.at_y(d)))
        else:
            a.append(net.send(part.at[lax.rem(z, 2), :, z // 2, :, first], z_got.at[n], p.at_z(d)))
            if both:
                b.append(net.send(part.at[:, y, :, :, second], y_got.at[n], p.at_y(d)))
    if flat:
        for k in range(4):
            a_own.append(net.load(part.at[chunk_rows(k, p.z, rows), first], z_sum.at[k]))
            if both:
                b_own.append(net.load(part.at[chunk_rows(p.y, k, rows), second], y_sum.at[k % 2, k // 2]))
    else:
        a_own.append(net.load(part.at[p.zl, :, p.zh, :, first], z_sum))
        if both:
            b_own.append(net.load(part.at[:, p.y, :, :, second], y_sum))

    yield
    for copy in a_own:
        copy.wait()
    for copy in a:
        copy.wait_recv()
    for y in range(4):
        t = z_sum[y].astype(F32)
        for n in range(3):
            t = t + z_got[n, y].astype(F32)
        z_sum[y] = t.astype(BF16)
    a = [
        net.send(z_sum.at[lax.rem(p.y + d, 4)], z_last.at[n], p.at_y(d)) for n, d in enumerate(order)
    ]
    if both:
        yield
        for copy in b_own:
            copy.wait()
        for copy in b:
            copy.wait_recv()
        for zl in range(2):
            for zh in range(2):
                t = y_sum[zl, zh].astype(F32)
                for n in range(3):
                    t = t + y_got[n, zl, zh].astype(F32)
                y_sum[zl, zh] = t.astype(BF16)
        b = []
        for n, d in enumerate(order):
            z = lax.rem(p.z + d, 4)
            b.append(net.send(y_sum.at[lax.rem(z, 2), z // 2], y_last.at[n], p.at_z(d)))
    yield
    for copy in a:
        copy.wait_recv()
    t = z_sum[p.y].astype(F32)
    for n in range(3):
        t = t + z_last[n].astype(F32)
    out[:, first] = t.astype(out.dtype)
    if both:
        yield
        for copy in b:
            copy.wait_recv()
        t = y_sum[p.zl, p.zh].astype(F32)
        for n in range(3):
            t = t + y_last[n].astype(F32)
        out[:, second] = t.astype(out.dtype)


SCATTER_GROUPS_LOADS = 2
SCATTER_GROUPS_FLAT_LOADS = 8
SCATTER_GROUPS = 12
SCATTER_GROUPS_FLAT = 30


def scatter_groups_scratch(r, cuts):
    a, b = cuts[1] - cuts[0], max(cuts[2] - cuts[1], HD)
    return [
        pltpu.VMEM((3, 4, r, a), BF16),
        pltpu.VMEM((4, r, a), BF16),
        pltpu.VMEM((3, r, a), BF16),
        pltpu.VMEM((3, 2, 2, r, b), BF16),
        pltpu.VMEM((2, 2, r, b), BF16),
        pltpu.VMEM((3, r, b), BF16),
    ]


def sems(remote, local):
    return [
        pltpu.SemaphoreType.DMA((remote,)),
        pltpu.SemaphoreType.DMA((remote,)),
        pltpu.SemaphoreType.DMA((max(local, 1),)),
    ]


def params(collective_id):
    return pltpu.CompilerParams(
        collective_id=collective_id, has_side_effects=True, vmem_limit_bytes=VM
    )


EPS_NORM = 1e-05
EPS_UNIT = 1e-06
SHAPE = jax.ShapeDtypeStruct


def all_to_team(net, packs, got):
    p = net.place
    me = 2 * p.x + p.c
    net.keep(packs.at[me], got.at[me])
    copies = []
    for d in (2, 1, 3, 0):
        for k in (1, 0):
            if d + k:
                to = 2 * p.chip(d) + lax.rem(p.c + k, 2)
                copies.append(net.send(packs.at[to], got.at[me], p.at_xc(d, k)))
    yield
    for copy in copies:
        copy.wait_recv()


TO_TEAM = 7


def swap_rows(net, pairs):
    p = net.place
    copies = []
    for src, dst in pairs:
        net.keep(src.at[p.zh], dst.at[p.zh])
        copies.append(net.send(src.at[1 - p.zh], dst.at[p.zh], p.at_z(2)))
    yield
    for copy in copies:
        copy.wait_recv()


def thin_rows(rows, padded):
    out = lax.broadcasted_iota(jnp.int32, (8 * rows, 8 * padded), 0)
    at = lax.broadcasted_iota(jnp.int32, (8 * rows, 8 * padded), 1)
    return ((out // rows == at // padded) & (out % rows == at % padded)).astype(BF16)


HEADS_W, SMALL_W = 8 * HD, HD
EXT_W = HEADS_W + SMALL_W
OUT_B, OUT_A = EXT_W, EXT_W + HD
WHOLE_W = EXT_W + 2 * HD
SHARED_W = 3 * HD
FIRST_W = 5 * HD + SHARED_W
PIECE = 32


def shift_pieces(tiles):
    lane = lax.broadcasted_iota(jnp.int32, tiles[0][0].shape, 1) // PIECE
    total = None
    for n, (tile, piece) in enumerate(tiles):
        turn = (PIECE * (n - piece)) % HD
        moved = pltpu.roll(tile, turn, 1) if turn else tile
        total = moved if total is None else jnp.where(lane == n, moved, total)
    return total


def pack_weights(kinds, gate_up, small, packs):
    share = small.shape[0]
    packs[...] = jnp.zeros_like(packs)
    for t in range(8):
        own, middle = 3 * (t // 2) + 2 * (t % 2), 3 * (t // 2) + 1
        parts = [w[:, own * HD : (own + 1) * HD] for w in kinds]
        shared = [w[:, middle * HD : (middle + 1) * HD] for w in kinds]
        shared = shared[:3] if t % 2 == 0 else [shared[3], small[...], shared[4]]
        for n, part in enumerate(parts + shared):
            packs[t, :share, n * HD : (n + 1) * HD] = part
    for n, w in enumerate(gate_up):
        for t in range(8):
            for j in range(4):
                tiles = []
                for e in range(4 * j, 4 * j + 4):
                    at = (2 * e + t // 4) * HD
                    tiles.append((w[:, at : at + HD].astype(F32), t % 4))
                at = FIRST_W + n * 4 * HD + j * HD
                packs[t, :share, at : at + HD] = shift_pieces(tiles).astype(BF16)


def start_kernel(wq, wk, wv, wp, wo, gate, up, small, tokens, grad_out, x_rows, g_rows, x_all, whole, own_ffn, packs, got, own, *sem):
    net = Net(*sem)
    p = net.place
    share = small.shape[0]
    pack_weights((wq, wk, wv, wp, wo), (gate, up), small, packs)
    first, second = pl.ds(0, FIRST_W), pl.ds(FIRST_W, own.shape[1] - FIRST_W)
    meet(team_all(p) + group_peers(p))
    trades = [all_to_team(net, packs.at[:, :, part], got.at[:, :, part]) for part in (first, second)]
    swaps = [swap_rows(net, (pair,)) for pair in ((tokens, x_rows), (grad_out, g_rows))]
    for n in range(2):
        next(trades[n])
        next(swaps[n])
    pick = thin_rows(share, packs.shape[1])

    def thin(part):
        wide = got[:, :, part].reshape(pick.shape[1], part.size)
        own[:, part] = mm(pick, wide).astype(BF16)

    interleave(trades[0])
    net.settle()
    thin(first)
    shared = pl.ds(pl.multiple_of(4 * HD + p.c * SHARED_W, HD), SHARED_W)
    heads = gather_groups(
        net,
        own,
        whole,
        [(pl.ds(0, 4 * HD), pl.ds(0, 4 * HD))],
        [(pl.ds(4 * HD, HD), pl.ds(OUT_A, HD)), (pl.ds(5 * HD, SHARED_W), shared)],
        True,
    )
    next(heads)
    interleave(swaps[0])
    x_team = gather_team(net, x_rows, x_all)
    next(x_team)
    for _ in range(3):
        next(heads)
    next(x_team)
    interleave(trades[1])
    thin(second)
    net.keep(own.at[:, second], own_ffn)
    interleave(x_team, heads, swaps[1])
    net.finish()


def start(kinds, gate, up, small, tokens, grad_out):
    share, width = kinds[0].shape
    two, n, _ = tokens.shape
    rows = SHAPE(tokens.shape, BF16)
    cols = FIRST_W + gate.shape[1] // 4
    return pl.pallas_call(
        start_kernel,
        out_shape=[
            rows,
            rows,
            SHAPE((two, 8, n, width), BF16),
            SHAPE((width, WHOLE_W), BF16),
            SHAPE((8 * share, cols - FIRST_W), BF16),
        ],
        in_specs=[VMEM] * 8 + [ANY] * 2,
        out_specs=[ANY] * 5,
        scratch_shapes=[
            pltpu.VMEM((8, 16, cols), BF16),
            pltpu.VMEM((8, 16, cols), BF16),
            pltpu.VMEM((8 * share, cols), BF16),
        ]
        + sems(2 * TO_TEAM + 2 + GATHER_TEAM + 3 * GATHER_GROUPS // 2 + 16, 9),
        compiler_params=params(1),
        name="start",
    )(*kinds, gate, up, small, tokens, grad_out)


def lanes(at):
    return pl.ds(pl.multiple_of(at * HD, HD), HD)


def trade_out(net, whole, w_out):
    p = net.place
    copies, own = [], []
    for d in (2, 1, 3, 0):
        for k in (1, 0):
            xd, cd = p.chip(d), lax.rem(p.c + k, 2)
            row_a, row_b = lanes(3 * xd + 2 * cd), lanes(3 * xd + 1)
            row_c = lanes(3 * xd + jnp.where(p.c == 0, 2 * cd, 1))
            col_a, col_b = lanes(3 * p.x + 2 * p.c), lanes(3 * p.x + 1)
            moves = (
                (whole.at[row_a, pl.ds(OUT_A, HD)], w_out.at[pl.ds(0, HD), col_a]),
                (whole.at[row_b, pl.ds(OUT_A, HD)], w_out.at[pl.ds(HD, HD), col_a]),
                (whole.at[row_c, pl.ds(OUT_B, HD)], w_out.at[lanes(p.c), col_b]),
            )
            for src, dst in moves:
                if d + k:
                    copies.append(net.send(src, dst, p.at_xc(d, k)))
                else:
                    own.append(net.load(src, dst))
    yield
    for copy in own:
        copy.wait()
    for copy in copies:
        copy.wait_recv()


def attn_fwd_kernel(x_all, whole, marks, drow, own_ffn, g_rows, *rest):
    kept, (w_ffn, g_all, w_out, part), rest = rest[:13], rest[13:17], rest[17:]
    bufs, (x_buf, w_buf, wo_buf, part_buf), rest = rest[:14], rest[14:18], rest[18:]
    normed, qkvp, raw, vec, mixed, gains, *saved, o = bufs
    net = Net(*rest[-3:])
    p = net.place
    loads = [net.load(whole.at[:, pl.ds(0, 9 * HD)], w_buf), net.load(x_all, x_buf)]
    meet(team_all(p) + group_peers(p))
    jobs = Jobs(
        gather_groups(net, own_ffn, w_ffn, *halves(own_ffn.shape[1])),
        trade_out(net, whole, wo_buf),
        gather_team(net, g_rows, g_all),
    )
    jobs.step(0, 1, 2)
    for copy in loads:
        copy.wait()
    project(x_buf, w_buf, gains, normed, qkvp, raw)
    for n in (0, 1, 2, 5):
        net.keep(bufs[n], kept[n])
    steps = [(0, 0, 0), (), (), (), (2,), ()]
    poke = lambda: jobs.step(*steps.pop(0)) if steps else None
    for s, head in enumerate(heads_here()):
        cols = pl.ds(s * HD, HD)
        poke()
        fwd_slot(poke, s, head, w_buf.at[:, pl.ds(8 * HD, HD)], marks, drow, qkvp, raw, vec, o, *saved, *rest[:-3])
        net.keep(vec.at[:, cols], kept[3].at[:, cols])
        for src, dst in zip(saved, kept[6:]):
            net.keep(src.at[s], dst.at[s])
    mixed[:, :HD] = o[:, :HD].astype(BF16)
    mixed[:, HD:] = jnp.where(p.c == 0, o[:, HD:], 0.0).astype(BF16)
    net.keep(mixed, kept[4])
    jobs.step(1, 1)
    net.keep(wo_buf, w_out)
    two, _, n, width = part.shape
    for h in range(two):
        for t in range(0, 8, 4):
            at = (h * 8 + t) * n
            y = mm(mixed[at : at + 4 * n, :], wo_buf[...]).astype(BF16)
            part_buf[h, t : t + 4] = y.reshape(4, n, width)
    net.keep(part_buf, part)
    jobs.drain()
    net.finish()


def attn_fwd(x_all, whole, marks, drow, own_ffn, g_rows):
    rows, cols = own_ffn.shape
    two, n, width = g_rows.shape
    kept = fwd_shapes(width)
    part = (two, 8, n, width)
    return pl.pallas_call(
        attn_fwd_kernel,
        out_shape=[SHAPE(*a) for a in kept]
        + [SHAPE((16 * rows, cols), BF16), SHAPE(part, BF16), SHAPE((2 * HD, width), BF16), SHAPE(part, BF16)],
        in_specs=[ANY, ANY, VMEM, VMEM, ANY, ANY],
        out_specs=[ANY] * (len(kept) + 4),
        scratch_shapes=[pltpu.VMEM(*a) for a in kept]
        + [
            pltpu.VMEM((SEQ, 2 * HD), F32),
            pltpu.VMEM((SEQ, width), BF16),
            pltpu.VMEM((width, 9 * HD), BF16),
            pltpu.VMEM((2 * HD, width), BF16),
            pltpu.VMEM(part, BF16),
        ]
        + fwd_scratch()
        + sems(GATHER_TEAM + GATHER_GROUPS + 21, 2 + 6 + 4 + 18 + 3),
        compiler_params=params(7),
        name="attn_fwd",
    )(x_all, whole, marks, drow, own_ffn, g_rows)


def norm_back(v, gain, d_normed):
    scale = lax.rsqrt(jnp.mean(v * v, axis=-1, keepdims=True) + EPS_NORM)
    unit = v * scale
    d_unit = d_normed * gain
    d_v = scale * (d_unit - unit * jnp.mean(d_unit * unit, axis=-1, keepdims=True))
    return d_v, d_normed * unit


def by_group(a):
    return a.reshape(2, 4, 2, a.shape[0] // 16, a.shape[1])


class TeamBlocks:
    def __init__(self, net, own, out):
        self.net, self.own, self.out = net, own, out

    def start(self):
        net, p, out = self.net, self.net.place, self.out
        place = out.at[:, 2 * p.x + p.c]
        self.to_r = net.send(self.own, place, p.at_x(1))
        self.to_l = net.send(self.own, place, p.at_x(3))
        self.shared = net.send(self.own, place, p.sibling())
        self.kept = net.load(self.own, place)

    def mine(self):
        self.kept.wait()
        self.shared.wait_recv()

    def hand_on(self):
        net, p, out = self.net, self.net.place, self.out
        left, right = 2 * p.chip(3) + p.c, 2 * p.chip(1) + p.c
        self.to_r.wait_recv()
        self.on_r = net.send(out.at[0, left], out.at[0, left], p.at_x(1))
        self.from_l = net.send(out.at[:, left], out.at[:, left], p.sibling())
        self.to_l.wait_recv()
        self.on_l = net.send(out.at[1, right], out.at[1, right], p.at_x(3))
        self.from_r = net.send(out.at[:, right], out.at[:, right], p.sibling())

    def opposite(self):
        net, p, out = self.net, self.net.place, self.out
        far = 2 * p.chip(2) + p.c
        self.far = []
        for n, copy in enumerate((self.on_r, self.on_l)):
            copy.wait_recv()
            self.far.append(net.send(out.at[n, far], out.at[n, far], p.sibling()))


class TeamSum:
    def __init__(self, net, part, got, total, from_l, from_r, all_l, all_r):
        self.net, self.part, self.got, self.total = net, part, got, total
        self.from_l, self.from_r, self.all_l, self.all_r = from_l, from_r, all_l, all_r
        self.swaps, self.last = {}, []

    def ready(self, d):
        p = self.net.place
        at = p.chip(d)
        self.swaps[d] = self.net.send(
            self.part.at[:, 2 * at + 1 - p.c], self.got.at[:, at], p.sibling()
        )

    def pair(self, d):
        p = self.net.place
        at = p.chip(d)
        self.swaps[d].wait_recv()
        self.total[:, at] = add(self.part[:, 2 * at + p.c], self.got[:, at])
        return at

    def near(self):
        net, p = self.net, self.net.place
        self.x_r = self.pair(1)
        self.last.append(net.send(self.total.at[1, self.x_r], self.all_l.at[1], p.at_x(1)))
        self.x_l = self.pair(3)
        self.last.append(net.send(self.total.at[0, self.x_l], self.all_r.at[0], p.at_x(3)))

    def far(self):
        net, p = self.net, self.net.place
        x_2 = self.pair(2)
        self.half_r = net.send(self.total.at[0, x_2], self.from_l, p.at_x(1))
        self.half_l = net.send(self.total.at[1, x_2], self.from_r, p.at_x(3))

    def on(self):
        net, p = self.net, self.net.place
        self.half_r.wait_recv()
        self.total[0, self.x_r] = add(self.total[0, self.x_r], self.from_l[...])
        self.last.append(net.send(self.total.at[0, self.x_r], self.all_l.at[0], p.at_x(1)))
        self.half_l.wait_recv()
        self.total[1, self.x_l] = add(self.total[1, self.x_l], self.from_r[...])
        self.last.append(net.send(self.total.at[1, self.x_l], self.all_r.at[1], p.at_x(3)))

    def result(self):
        for copy in self.last:
            copy.wait_recv()
        mine = self.total[:, self.net.place.x].astype(F32)
        return mine + self.all_l[...].astype(F32) + self.all_r[...].astype(F32)


def ffn_kernel(cuts, *refs):
    (part, x_rows, g_rows, gain, own_down, w_ffn, g_all), refs = refs[:7], refs[7:]
    (hidden, d_hidden, d_gain, branch_all, out_part, ffn_sum, down_out), refs = refs[:7], refs[7:]
    (w_in, w_down, g_buf, nf_all, normed, act, d_in, back, branch, d_ffn, d_down, out_buf), refs = refs[:12], refs[12:]
    scratch = [refs[6 * n : 6 * n + 6] for n in range(5)]
    net = Net(*refs[-3:])
    p = net.place
    loads = [net.load(w_ffn, w_in), net.load(g_all, g_buf)]
    meet(team_peers(p) + group_peers(p))
    two, _, n, width = part.shape
    half = w_down.shape[0]
    pieces = [pl.ds(m * n // 2, n // 2) for m in range(2)]

    def finish_rows(piece):
        def finish(sums):
            h = x_rows[:, piece].astype(F32) + sums
            hidden[:, piece] = h
            scale = lax.rsqrt(jnp.mean(h * h, axis=-1, keepdims=True) + EPS_NORM)
            normed[:, piece] = (h * scale * gain[1:2, :][None]).astype(BF16)

        return finish

    jobs = Jobs(
        *[
            scatter_team(net, part.at[:, :, piece], *scratch[m], finish_rows(piece))
            for m, piece in enumerate(pieces)
        ],
        gather_groups(net, own_down, w_down, *halves(width)),
    )
    blocks = [TeamBlocks(net, normed.at[:, piece], nf_all.at[:, :, piece]) for piece in pieces]
    jobs.step(0, 1, 2, 0, 1, 2, 2, 2, 0, 1)
    for m in range(2):
        jobs.step(m)
        blocks[m].start()
    jobs.drain()
    for copy in loads:
        copy.wait()
    net.settle()
    sums = [
        TeamSum(net, back.at[:, :, piece], *scratch[2 + m]) for m, piece in enumerate(pieces)
    ]

    def flat(ref, at):
        return ref[:, pl.ds(2 * at, 2)].reshape(4 * n, ref.shape[3])

    def work(d):
        at = p.chip(d)
        pre = mm(flat(nf_all, at), w_in[...])
        gate, up = pre[:, :half], pre[:, half:]
        sig = jax.nn.sigmoid(gate)
        silu = gate * sig
        act[:, pl.ds(2 * at, 2)] = (silu * up).astype(BF16).reshape(two, 2, n, half)
        d_act = mm_nt(flat(g_buf, at), w_down[...])
        d_gate = (d_act * up * (sig + silu * (1.0 - sig))).astype(BF16)
        d_up = (d_act * silu).astype(BF16)
        d_pre = jnp.concatenate([d_gate, d_up], axis=1)
        d_in[:, pl.ds(2 * at, 2)] = d_pre.reshape(two, 2, n, 2 * half)
        back[:, pl.ds(2 * at, 2)] = mm_nt(d_pre, w_in[...]).astype(BF16).reshape(two, 2, n, width)
        for s in sums:
            s.ready(d)

    for b in blocks:
        b.mine()
    work(0)
    for b in blocks:
        b.hand_on()
    for b in blocks:
        b.from_l.wait_recv()
    work(3)
    for b in blocks:
        b.opposite()
    for b in blocks:
        b.from_r.wait_recv()
    work(1)
    for s in sums:
        s.near()
    for b in blocks:
        for copy in b.far:
            copy.wait_recv()
    work(2)
    for s in sums:
        s.far()
    for s in sums:
        s.pair(0)
    rows = two * 8 * n
    step = width // 4
    for k in range(4):
        cols = slice(k * step, (k + 1) * step)
        left = nf_all[:, :, :, cols].reshape(rows, step)
        d_ffn[cols, :] = mm_tn(left, d_in[...].reshape(rows, 2 * half)).astype(BF16)
        if k in (1, 2):
            sums[k - 1].on()
    group = scatter_groups(net, d_ffn, ffn_sum, cuts, *scratch[4])
    next(group)
    d_gain[...] = jnp.zeros_like(d_gain)
    teams = []
    for s, piece in zip(sums, pieces):
        d_h, d_g = norm_back(hidden[:, piece], gain[1:2, :][None], s.result())
        d_h = d_h + g_rows[:, piece].astype(F32)
        d_hidden[:, piece] = d_h
        branch[:, piece] = d_h.astype(BF16)
        d_gain[...] += jnp.sum(jnp.sum(d_g, axis=0), axis=0, keepdims=True)
        teams.append(gather_team(net, branch.at[:, piece], branch_all.at[:, :, piece]))
        next(teams[-1])
    step = half // 2
    for k in range(2):
        cols = slice(k * step, (k + 1) * step)
        left = act[:, :, :, cols].reshape(rows, step)
        d_down[cols, :] = mm_tn(left, g_buf[...].reshape(rows, width)).astype(BF16)
    net.keep(d_down, down_out)
    for h in range(two):
        for t in range(0, 8, 4):
            left = act[h, t : t + 4].reshape(4 * n, half)
            out_buf[h, t : t + 4] = mm(left, w_down[...]).astype(BF16).reshape(4, n, width)
    net.keep(out_buf, out_part)
    for team in teams:
        next(team)
    next(group)
    next(group)
    jobs = Jobs(*teams, group)
    jobs.drain()
    net.finish()


def ffn(part, x_rows, g_rows, gain, own_down, w_ffn, g_all):
    two, n, width = x_rows.shape
    cols = w_ffn.shape[1]
    half, rows = cols // 2, own_down.shape[0]
    every = (two, 8, n, width)
    share = width // 16
    cuts = (0, half, cols)
    return pl.pallas_call(
        functools.partial(ffn_kernel, cuts),
        out_shape=[
            SHAPE((two, n, width), F32),
            SHAPE((two, n, width), F32),
            SHAPE((1, width), F32),
            SHAPE(every, BF16),
            SHAPE(every, BF16),
            SHAPE((share, cols), BF16),
            SHAPE((16 * rows, width), BF16),
        ],
        in_specs=[ANY, VMEM, VMEM, VMEM, ANY, ANY, ANY],
        out_specs=[VMEM, VMEM, VMEM, ANY, ANY, VMEM, ANY],
        scratch_shapes=[
            pltpu.VMEM((width, cols), BF16),
            pltpu.VMEM((half, width), BF16),
            pltpu.VMEM(every, BF16),
            pltpu.VMEM(every, BF16),
            pltpu.VMEM((two, n, width), BF16),
            pltpu.VMEM((two, 8, n, half), BF16),
            pltpu.VMEM((two, 8, n, cols), BF16),
            pltpu.VMEM(every, BF16),
            pltpu.VMEM((two, n, width), BF16),
            pltpu.VMEM((width, cols), BF16),
            pltpu.VMEM((half, width), BF16),
            pltpu.VMEM(every, BF16),
        ]
        + scatter_team_scratch(n // 2, width) * 4
        + scatter_groups_scratch(share, cuts)
        + sems(
            4 * SCATTER_TEAM + 4 * GATHER_TEAM + GATHER_GROUPS + SCATTER_GROUPS_FLAT,
            2 + 2 * SCATTER_TEAM_LOADS + 2 + 2 + 2 + 2 + SCATTER_GROUPS_FLAT_LOADS,
        ),
        compiler_params=params(3),
        name="ffn",
    )(part, x_rows, g_rows, gain, own_down, w_ffn, g_all)


def trade_out_back(net, d_out, whole):
    p = net.place
    rows, middle, own = [], [], []
    cases = [(d, k) for d in (2, 1, 3, 0) for k in (1, 0)]
    for d, k in cases:
        xd, cd = p.chip(d), lax.rem(p.c + k, 2)
        for side, col in enumerate((lanes(3 * xd + 2 * cd), lanes(3 * xd + 1))):
            src = d_out.at[pl.ds(0, HD), col]
            dst = whole.at[lanes(3 * p.x + 2 * p.c), pl.ds(side * HD, HD)]
            if d + k:
                rows.append(net.send(src, dst, p.at_xc(d, k)))
            else:
                own.append(net.local(src, dst))
                own[-1].start()
    for d, k in cases:
        xd, cd = p.chip(d), lax.rem(p.c + k, 2)
        for side, col in enumerate((lanes(3 * xd + 2 * cd), lanes(3 * xd + 1))):
            src = d_out.at[pl.ds(HD, HD), col]
            dst = whole.at[lanes(3 * p.x + 1), pl.ds(side * HD, HD)]
            if d + k:
                middle.append((k, net.prepare(src, dst, p.at_xc(d, k))))
            else:
                middle.append((-1, net.local(src, dst)))

    @pl.when(p.c == 0)
    def _():
        for _, copy in middle:
            copy.start()

    yield
    for copy in rows:
        copy.wait_recv()
    for copy in own:
        copy.wait()
    for core in range(2):

        @pl.when(p.c == core)
        def _(core=core):
            for k, copy in middle:
                if k == core:
                    copy.wait_recv()

    @pl.when(p.c == 0)
    def _():
        for k, copy in middle:
            if k < 0:
                copy.wait()
            else:
                copy.wait_send()

    yield


TRADE_BACK = 28


def back_kernel(cuts, *refs):
    (marks, gains, d_gain_f, x_rows, hidden, d_hidden, ffn_sum), refs = refs[:7], refs[7:]
    (whole, w_out, mixed, normed, branch, part_o, d_down), refs = refs[:7], refs[7:]
    given, refs = refs[:10], refs[10:]
    (output, d_tokens, got_heads, got_rest, down_sum), refs = refs[:5], refs[5:]
    bufs, refs = refs[:10], refs[10:]
    (w_buf, wo_buf, mixed_buf, normed_buf, rows_buf, do, d_out, d_ext, d_conv), refs = refs[:9], refs[9:]
    (d_head_a, d_head_b, d_small, turned, trade, out_rows, d_rows), refs = refs[:7], refs[7:]
    (sum_a, sum_b, sum_s, sum_o, packs_heads, packs_rest), refs = refs[:6], refs[6:]
    own, refs = refs[:7], refs[7:]
    scratch = [refs[6 * n : 6 * n + 6] for n in range(7)]
    net = Net(*refs[-3:])
    p = net.place
    qkvp, raw, vec, *saved = bufs
    two, _, n, width = rows_buf.shape
    rows = two * 8 * n
    first = [net.load(w_out, wo_buf), net.load(branch, rows_buf), net.load(mixed, mixed_buf)]
    second = [net.load(given[m], bufs[m]) for m in (0,)]
    second.append(net.load(given[3].at[0], bufs[3].at[0]))
    meet(team_all(p) + group_peers(p))

    def finish(sums):
        out_rows[...] = (hidden[...] + sums).astype(BF16)

    def out_grad():
        yield from trade_out_back(net, d_out, trade)
        yield from scatter_groups(net, trade, sum_o, cuts[1], *scratch[0])

    def output_rows():
        yield from scatter_team(net, part_o, *scratch[1], finish)
        yield from swap_rows(net, ((out_rows, output),))

    jobs = Jobs(
        output_rows(), out_grad(), scatter_groups(net, d_down, down_sum, cuts[0], *scratch[2])
    )
    jobs.step(0)
    for copy in first:
        copy.wait()
    third = [net.load(given[m].at[0], bufs[m].at[0]) for m in range(4, 10)]
    third += [net.load(given[m], bufs[m]) for m in (1, 2)]
    third.append(net.load(whole.at[:, pl.ds(0, EXT_W)], w_buf))
    branch_rows = rows_buf[...].reshape(rows, width)
    d_mixed = mm_nt(branch_rows, wo_buf[...])
    do[:, :HD] = d_mixed[:, :HD]
    do[:, HD:] = jnp.where(p.c == 0, d_mixed[:, HD:], 0.0)
    d_out[...] = mm_tn(mixed_buf[...], branch_rows).astype(BF16)
    jobs.step(1, 2)
    fourth = [net.load(normed, normed_buf)]
    later = []
    for copy in second:
        copy.wait()
    waits = [third, None, None, None, later, None, None, None]
    steps = [(0,), (), (), (0,), (2, 2), (), (1,), (1,)]

    def poke():
        jobs.step(*steps.pop(0))
        for copy in waits.pop(0) or ():
            copy.wait()
        if len(steps) == 7:
            fourth.append(net.load(given[3].at[1], bufs[3].at[0]))

    side = 4 * HD
    d_raw = 0.0
    sums_a = scatter_groups(net, d_head_a, sum_a, cuts[2], *scratch[3])
    sums_b = scatter_groups(net, d_head_b, sum_b, cuts[2], *scratch[4])
    for s, (head, grads, job) in enumerate(zip(heads_here(), (d_head_a, d_head_b), (sums_a, sums_b))):
        d_raw = d_raw + bwd_slot(
            poke, s, head, qkvp, raw, w_buf.at[:, pl.ds(HEADS_W, HD)], marks, vec, mixed_buf, do, *saved, d_ext, d_conv, *own
        )
        if s == 0:
            later += [net.load(given[m].at[1], bufs[m].at[0]) for m in range(4, 10)]
            for copy in fourth:
                copy.wait()
        for k in range(4):
            part = slice(k * width // 4, (k + 1) * width // 4)
            grads[part, :] = mm_tn(normed_buf[:, part], d_ext[:, s * side : (s + 1) * side]).astype(BF16)
        next(job)
        poke()
    d_ext[:, HEADS_W:] = d_raw.astype(d_ext.dtype)
    next(sums_a)
    next(sums_a)

    sums = TeamSum(net, rows_buf, *scratch[5])
    turned[...] = jnp.zeros_like(turned)

    def work(d):
        at = p.chip(d)
        total = 0.0
        for h in range(two):
            here = pl.ds(pl.multiple_of((h * 8 + 2 * at) * n, 2 * n), 2 * n)
            y = mm_nt(d_ext[here, :], w_buf[...])
            total = total + jnp.sum(y * normed_buf[here, :].astype(F32), axis=0, keepdims=True)
            rows_buf[h, pl.ds(2 * at, 2)] = y.astype(BF16).reshape(2, n, width)
        turned[0:1, :] += total
        sums.ready(d)

    work(2)
    work(1)
    sums.far()
    work(3)
    sums.near()
    work(0)
    sums.pair(0)
    head_a, head_b = heads_here()
    turned[0:1, :] = turned[0:1, :] / gains[0:1, :]
    turned[1:2, :] = d_gain_f[...]
    turned[CONV_AT : CONV_AT + TAPS, lanes(head_a)] = d_conv[0, :TAPS, :]
    turned[CONV_AT : CONV_AT + TAPS, lanes(head_b)] = d_conv[1, :TAPS, :]
    for k in range(width // HD):
        part = slice(k * HD, (k + 1) * HD)
        t = mm_tn(normed_buf[:, part], d_ext[:, HEADS_W:]) + turned[:, part].T
        d_small[part, :] = t.astype(BF16)
    sums_s = scatter_groups(net, d_small, sum_s, cuts[3], *scratch[6])
    next(sums_s)
    next(sums_b)
    next(sums_b)
    sums.on()
    jobs.step(0, 1, 1)
    Jobs(sums_a).drain()
    jobs.drain()
    eight, padded, _ = packs_heads.shape
    spread = thin_rows(sum_a.shape[0] // eight, padded).T

    def pack(part, packs, at):
        wide = mm(spread, part[...]).astype(BF16)
        packs[:, :, at : at + part.shape[1]] = wide.reshape(eight, padded, part.shape[1])

    pack(sum_a, packs_rest, 0)
    pack(sum_o, packs_rest, side)
    pack(ffn_sum, packs_rest, side + 2 * HD)
    rest = all_to_team(net, packs_rest, got_rest)
    next(rest)
    next(sums_s)
    d_x, _ = norm_back(x_rows[...].astype(F32), gains[0:1, :][None], sums.result())
    d_rows[...] = (d_x + d_hidden[...]).astype(BF16)
    swaps = swap_rows(net, ((d_rows, d_tokens),))
    next(swaps)
    Jobs(sums_b, sums_s).drain()
    pack(sum_b, packs_heads, 0)
    pack(sum_s, packs_heads, side)
    interleave(all_to_team(net, packs_heads, got_heads), swaps, rest)
    net.finish()


def back(values, arrays, given):
    marks, gains, d_gain_f, x_rows, hidden, d_hidden, ffn_sum = values
    whole, w_out, mixed, normed, branch, part_o, d_down = arrays
    two, n, width = hidden.shape
    r = width // 16
    down = d_down.shape[0] // 16
    side = 4 * HD
    ffn_w = ffn_sum.shape[1]
    cuts = [(0, width // 2, width), (0, HD, 2 * HD), (0, side // 2, side), (0, HD, HD)]
    rows = SHAPE((two, n, width), BF16)
    packs = [(8, 16, side + HD), (8, 16, side + 2 * HD + ffn_w)]
    vmem = pltpu.VMEM
    return pl.pallas_call(
        functools.partial(back_kernel, cuts),
        out_shape=[rows, rows] + [SHAPE(a, BF16) for a in packs] + [SHAPE((down, width), F32)],
        in_specs=[VMEM] * 7 + [ANY] * (7 + len(given)),
        out_specs=[ANY] * 4 + [VMEM],
        scratch_shapes=[vmem((1,) + a.shape[1:] if m > 2 else a.shape, a.dtype) for m, a in enumerate(given)]
        + [
            vmem((width, EXT_W), BF16),
            vmem(w_out.shape, BF16),
            vmem(mixed.shape, BF16),
            vmem(normed.shape, BF16),
            vmem(branch.shape, BF16),
            vmem((SEQ, 2 * HD), F32),
            vmem((2 * HD, width), BF16),
            vmem((SEQ, EXT_W), BF16),
            vmem((2, 8, HD), F32),
            vmem((width, side), BF16),
            vmem((width, side), BF16),
            vmem((width, HD), BF16),
            vmem((HD, width), F32),
            vmem((width, 2 * HD), BF16),
            vmem((two, n, width), BF16),
            vmem((two, n, width), BF16),
            vmem((r, side), BF16),
            vmem((r, side), BF16),
            vmem((r, HD), BF16),
            vmem((r, 2 * HD), BF16),
        ]
        + [vmem(a, BF16) for a in packs]
        + bwd_scratch()
        + scatter_groups_scratch(r, cuts[1])
        + scatter_team_scratch(n, width)
        + scatter_groups_scratch(down, cuts[0])
        + scatter_groups_scratch(r, cuts[2])
        + scatter_groups_scratch(r, cuts[2])
        + scatter_team_scratch(n, width)
        + scatter_groups_scratch(r, cuts[3])
        + sems(
            TRADE_BACK + 2 * SCATTER_TEAM + 4 * SCATTER_GROUPS_FLAT + 2 * SCATTER_GROUPS_FLAT + 2 + 2 * TO_TEAM,
            3 + 3 + 9 + 8 + 4 + SCATTER_TEAM_LOADS + 6 * SCATTER_GROUPS_FLAT_LOADS + 2 + 2,
        ),
        compiler_params=params(5),
        name="back",
    )(*values, *arrays, *given)


def unpack_kernel(heads, rest, rows_in, tokens_in, down_in, *outs):
    kinds, gate, up, small, rows, tokens, down = outs[:5], outs[5], outs[6], outs[7], outs[8], outs[9], outs[10]
    share = small.shape[0]
    side = 4 * HD
    for n, out in enumerate(kinds):
        for x in range(4):
            for j in range(3):
                t = 2 * x + j // 2
                if n < 4:
                    src, col = (heads, n * HD) if j == 1 else (rest, n * HD)
                else:
                    src, col = rest, side + (j % 2) * HD
                head = 3 * x + j
                out[:, head * HD : (head + 1) * HD] = src[t, :share, col : col + HD].astype(F32)
    total = heads[0, :, side : side + SMALL_W].astype(F32)
    for t in range(1, 8):
        total = total + heads[t, :, side : side + SMALL_W].astype(F32)
    small[...] = total[:share]
    for n, out in enumerate((gate, up)):
        for tile in range(32):
            e = tile // 2
            col = side + 2 * HD + n * 4 * HD + (e // 4) * HD
            parts = [
                (rest[t, :, col : col + HD].astype(F32), e % 4)
                for t in range(4 * (tile % 2), 4 * (tile % 2) + 4)
            ]
            out[:, tile * HD : (tile + 1) * HD] = shift_pieces(parts)[:share]
    rows[...] = rows_in[...]
    tokens[...] = tokens_in[...]
    down[...] = down_in[...]


def unpack(heads, rest, rows, tokens, down, share, ff):
    two, n, width = rows.shape
    return pl.pallas_call(
        unpack_kernel,
        out_shape=[SHAPE((share, width), F32)] * 5
        + [SHAPE((share, ff), F32)] * 2
        + [SHAPE((share, HD), F32)]
        + [SHAPE(rows.shape, BF16)] * 2
        + [SHAPE(down.shape, F32)],
        in_specs=[VMEM] * 5,
        out_specs=[VMEM] * 11,
        compiler_params=pltpu.CompilerParams(vmem_limit_bytes=VM),
        name="unpack",
    )(heads, rest, rows, tokens, down)


def per_device(
    tokens,
    doc_start,
    gain_attn,
    w_query,
    w_key,
    w_value,
    w_path,
    conv_path,
    w_beta,
    w_out,
    gain_ffn,
    w_gate,
    w_up,
    w_down,
    grad_out,
):
    zh = lax.axis_index("zh")
    width = tokens.shape[2]
    share = w_query.shape[0]
    small = jnp.concatenate([gain_attn[:, None], gain_ffn[:, None], conv_path.T, w_beta], axis=1)
    small = jnp.pad(small, ((0, 0), (0, SMALL_W - small.shape[1])))
    x_rows, g_rows, x_all, whole, own_ffn = start(
        (w_query, w_key, w_value, w_path, w_out), w_gate, w_up, small, tokens, grad_out
    )
    doc_rows = jnp.cumsum(doc_start, axis=1)
    docs = jnp.where(zh == 0, doc_rows[0], doc_rows[1]).astype(F32)
    marks = [docs]
    for tap in range(1, TAPS):
        same = docs[: SEQ - tap] == docs[tap:]
        marks.append(jnp.concatenate([jnp.zeros((tap,), F32), same.astype(F32)]))
    drow = jnp.stack(marks + marks)
    marks = drow.T

    normed, qkvp, raw, vec, mixed, gains, *saved, w_ffn, g_all, w_out_t, part = attn_fwd(
        x_all.reshape(SEQ, width), whole, marks, drow, own_ffn, g_rows
    )
    hidden, d_hidden, d_gain_f, branch_all, out_part, ffn_sum, d_down = ffn(
        part, x_rows, g_rows, gains, w_down, w_ffn, g_all
    )
    output, d_tokens, heads_back, rest_back, d_down = back(
        (marks, gains, d_gain_f, x_rows, hidden, d_hidden, ffn_sum),
        (whole, w_out_t, mixed, normed, branch_all, out_part, d_down),
        (qkvp, raw, vec, *saved),
    )
    *kinds, d_gate_w, d_up_w, small, output, d_tokens, d_down = unpack(
        heads_back, rest_back, output, d_tokens, d_down, share, w_gate.shape[1]
    )
    return (
        output,
        d_tokens,
        small[:, 0],
        *kinds[:4],
        small[:, 2:6].T,
        small[:, 6:18],
        kinds[4],
        small[:, 1],
        d_gate_w,
        d_up_w,
        d_down,
    )


def solution(mesh):
    names = ("zl", "y", "zh", "x", "c")
    fine = Mesh(mesh.devices.reshape(2, 4, 2, 4, 2), names)
    dp, ctx = names[:2], names[2:]
    rows, flat, mat, taps = P(dp, ctx, None), P(names), P(names, None), P(None, names)
    return jax.shard_map(
        per_device,
        mesh=fine,
        in_specs=(
            rows, P(dp, None), flat, mat, mat, mat, mat, taps, mat, mat, flat, mat, mat, mat, rows,
        ),
        out_specs=(
            rows, rows, flat, mat, mat, mat, mat, taps, mat, mat, flat, mat, mat, mat,
        ),
        check_vma=False,
    )
```

profile of v0, /device:TPU:1, one launch (start us, length us, event | category | flops | bytes accessed | tf_op | source)
XLA Modules:
  0.0 254.4 jit_solution(6383967365662390436)
XLA Ops:
  0.7 0.7 copy.49
  1.4 0.8 copy.48
  2.2 0.8 copy.50
  2.9 1.4 fusion.6.small
  4.3 0.7 copy.54
  5.0 0.6 reduce-window.6
  5.6 0.2 slice_reduce_fusion
  5.8 0.2 reduce-window.9
  6.0 0.1 broadcast_add_fusion
  6.1 0.1 slice_compare_fusion
  6.1 0.1 slice_compare_fusion.2
  6.2 0.1 slice_compare_fusion.1
  6.3 0.1 pad_convert_fusion.1
  6.4 0.1 add_convert_fusion
  6.4 0.1 pad_convert_fusion
  6.5 0.1 stack.32.drow
  6.6 0.0 copy-start
  6.6 1.0 copy.47
  7.6 47.9 %start.1 = (bf16[2,64,1536]{2,1,0:T(8,128)(2,1)}, bf16[2,64,1536]{2,1,0:T(8,128)(2,1)}, bf16[2,8,64,1536]{3,2,1,0:T(8,128)(2,1)}, bf16[1536,1408]{1,0:T(8,128)(2,1)}, bf16[96,1024]{1,0:T(8,128)(2,1)}) custom-call(bf16[12,1536]{1,0:T(8,128)(2,1)} %wq.1, bf16[12,1536]{1,0:T(8,128)(2,1)} %wk.1, bf16[12,1536]{1,0:T(8,128)(2,1)} %wv.1, bf16[12,1536]{1,0:T(8,128)(2,1)} %wp.1, ...), custom_call_target="tpu_custom_call" | custom-call | tf_op jit(solution)/shard_map/start/pallas_call | solution.py:866
  55.5 0.0 copy-done
  55.5 35.7 %attn_fwd.1 = (bf16[1024,1536]{1,0:T(8,128)(2,1)}, bf16[1024,1024]{1,0:T(8,128)(2,1)}, f32[1024,128]{1,0:T(8,128)}, bf16[1024,256]{1,0:T(8,128)(2,1)}, bf16[1024...) custom-call(bf16[1024,1536]{1,0:T(8,128)(2,1)} %bitcast.20, ...), custom_call_target="tpu_custom_call" | custom-call | tf_op jit(solution)/shard_map/attn_fwd/pallas_call | solution.py:967
  91.2 78.6 %ffn.1 = (f32[2,64,1536]{2,1,0:T(8,128)}, f32[2,64,1536]{2,1,0:T(8,128)}, f32[1,1536]{1,0:T(1,128)}, bf16[2,8,64,1536]{3,2,1,0:T(8,128)(2,1)}, bf16[2,8,64,1536]...) custom-call(bf16[2,8,64,1536]{3,2,1,0:T(8,128)(2,1)} %get-tuple-element.64.refs_0_, ...), custom_call_target="tpu_custom_call" | custom-call | tf_op jit(solution)/shard_map/ffn/pallas_call | solution.py:1215
  169.8 77.0 %back.1 = (bf16[2,64,1536]{2,1,0:T(8,128)(2,1)}, bf16[2,64,1536]{2,1,0:T(8,128)(2,1)}, bf16[8,16,640]{2,1,0:T(8,128)(2,1)}, bf16[8,16,1792]{2,1,0:T(8,128)(2,1)}, f32[32,1536]{1,0:T(8,128)}) custom-call(f32[1024,8]{1,0:T(8,128)} %bitcast.19, f32[8,1536]{1,0:T(8,128)} %get-tuple-element.63.refs_3_.refs_1_, f32[1,1536]{1,0:T(1,128)} %get-tuple-element.68.refs_2_, ...), custom_call_target="tpu_custom_call" | custom-call | tf_op jit(solution)/shard_map/back/pallas_call | solution.py:1465
  246.8 2.8 %unpack.1 = (f32[12,1536]{1,0:T(8,128)}, f32[12,1536]{1,0:T(8,128)}, f32[12,1536]{1,0:T(8,128)}, f32[12,1536]{1,0:T(8,128)}, f32[12,1536]{1,0:T(8,128)}, /*index...) custom-call(bf16[8,16,640]{2,1,0:T(8,128)(2,1)} %get-tuple-element.8, ...), custom_call_target="tpu_custom_call" | custom-call | tf_op jit(solution)/shard_map/unpack/pallas_call | solution.py:1545
  249.6 1.5 slice_reduce_fusion.1
  251.1 1.4 slice.56
  252.4 0.8 slice_bitcast_fusion
  253.2 0.7 copy.51
  (2 shorter events, 0.0 us)
Async XLA Ops:
  6.6 49.0 %copy-start = (f32[8,1024]{1,0:T(8,128)}, f32[8,1024]{1,0:T(8,128)S(1)}, u32[]{:S(2)}) copy-start(f32[8,1024]{1,0:T(8,128)S(1)} %stack.32.drow) | copy-start | bytes 98308
where the time goes:
time: 258 us; the launch traced here: 254 us
  Pallas kernels  242 us (94%)
  local copies, waits for them, and re-layouts  8.52 us (3%)
  other arithmetic  2.66 us (1%)
    pallas_call x1, Pallas kernels, ffn(): pl.pallas_call(functools.partial(ffn_kernel, cuts), out_shape=[SHAPE((two...  78.6 us
    pallas_call x1, Pallas kernels, back(): pl.pallas_call(functools.partial(back_kernel, cuts), out_shape=[rows, row...  77 us
    pallas_call x1, Pallas kernels, start(): pl.pallas_call(start_kernel, out_shape=[rows, rows, SHAPE((two, 8, n, wid...  47.9 us
    pallas_call x1, Pallas kernels, attn_fwd(): pl.pallas_call(attn_fwd_kernel, out_shape=[SHAPE(*a) for a in kept] + [SH...  35.7 us

commit v1 on v0

--- a/solution.py
+++ b/solution.py
@@ -793,6 +793,42 @@
     return total
 
 
+def small_columns(gain_a, gain_f, conv, w_beta, rows_buf, beta_buf):
+    share = w_beta.shape[0]
+    rows_buf[...] = jnp.zeros_like(rows_buf)
+    beta_buf[...] = jnp.zeros_like(beta_buf)
+    rows_buf[0:1, :share] = gain_a[...].astype(F32)
+    rows_buf[1:2, :share] = gain_f[...].astype(F32)
+    rows_buf[CONV_AT : CONV_AT + TAPS, :share] = conv[...].astype(F32)
+    beta_buf[:share, : w_beta.shape[1]] = w_beta[...].astype(F32)
+    columns = rows_buf[...].T[: beta_buf.shape[0], :]
+    return (columns + pltpu.roll(beta_buf[...], BETA_AT, 1))[:share].astype(BF16)
+
+
+def mark_documents(starts, zh, drow, marks):
+    row, col = iota2(0), iota2(1)
+    upto = (row <= col).astype(BF16)
+    starts = jnp.broadcast_to(starts[pl.ds(zh, 1), :].astype(F32), drow.shape)
+    before = 0.0
+    for k in range(NB):
+        cols = slice(k * BLK, (k + 1) * BLK)
+        docs = mm(starts[:, cols], upto) + before
+        before = docs[:, BLK - 1 :]
+        drow[:, cols] = docs
+    docs = drow[...]
+    lane = lax.broadcasted_iota(jnp.int32, docs.shape, 1)
+    kind = lax.broadcasted_iota(jnp.int32, docs.shape, 0) % TAPS
+    total = docs
+    for m in range(1, TAPS):
+        same = ((pltpu.roll(docs, m, 1) == docs) & (lane >= m)).astype(F32)
+        total = jnp.where(kind == m, same, total)
+    drow[...] = total
+    for k in range(NB):
+        cols = slice(k * BLK, (k + 1) * BLK)
+        tall = jnp.concatenate([total[:, cols]] * (BLK // total.shape[0]), axis=0)
+        marks[cols, :] = tall.T[:, : marks.shape[1]]
+
+
 def pack_weights(kinds, gate_up, small, packs):
     share = small.shape[0]
     packs[...] = jnp.zeros_like(packs)
@@ -800,7 +836,7 @@
         own, middle = 3 * (t // 2) + 2 * (t % 2), 3 * (t // 2) + 1
         parts = [w[:, own * HD : (own + 1) * HD] for w in kinds]
         shared = [w[:, middle * HD : (middle + 1) * HD] for w in kinds]
-        shared = shared[:3] if t % 2 == 0 else [shared[3], small[...], shared[4]]
+        shared = shared[:3] if t % 2 == 0 else [shared[3], small, shared[4]]
         for n, part in enumerate(parts + shared):
             packs[t, :share, n * HD : (n + 1) * HD] = part
     for n, w in enumerate(gate_up):
@@ -814,10 +850,11 @@
                 packs[t, :share, at : at + HD] = shift_pieces(tiles).astype(BF16)
 
 
-def start_kernel(wq, wk, wv, wp, wo, gate, up, small, tokens, grad_out, x_rows, g_rows, x_all, whole, own_ffn, packs, got, own, *sem):
+def start_kernel(wq, wk, wv, wp, wo, gate, up, gain_a, gain_f, conv, w_beta, starts, tokens, grad_out, x_rows, g_rows, x_all, whole, own_ffn, drow, marks, packs, got, own, rows_buf, beta_buf, *sem):
     net = Net(*sem)
     p = net.place
-    share = small.shape[0]
+    share = w_beta.shape[0]
+    small = small_columns(gain_a, gain_f, conv, w_beta, rows_buf, beta_buf)
     pack_weights((wq, wk, wv, wp, wo), (gate, up), small, packs)
     first, second = pl.ds(0, FIRST_W), pl.ds(FIRST_W, own.shape[1] - FIRST_W)
     meet(team_all(p) + group_peers(p))
@@ -845,6 +882,7 @@
         True,
     )
     next(heads)
+    mark_documents(starts, p.zh, drow, marks)
     interleave(swaps[0])
     x_team = gather_team(net, x_rows, x_all)
     next(x_team)
@@ -858,7 +896,7 @@
     net.finish()
 
 
-def start(kinds, gate, up, small, tokens, grad_out):
+def start(kinds, gate, up, gain_a, gain_f, conv, w_beta, starts, tokens, grad_out):
     share, width = kinds[0].shape
     two, n, _ = tokens.shape
     rows = SHAPE(tokens.shape, BF16)
@@ -871,18 +909,22 @@
             SHAPE((two, 8, n, width), BF16),
             SHAPE((width, WHOLE_W), BF16),
             SHAPE((8 * share, cols - FIRST_W), BF16),
+            SHAPE((8, SEQ), F32),
+            SHAPE((SEQ, 8), F32),
         ],
-        in_specs=[VMEM] * 8 + [ANY] * 2,
-        out_specs=[ANY] * 5,
+        in_specs=[VMEM] * 12 + [ANY] * 2,
+        out_specs=[ANY] * 5 + [VMEM] * 2,
         scratch_shapes=[
             pltpu.VMEM((8, 16, cols), BF16),
             pltpu.VMEM((8, 16, cols), BF16),
             pltpu.VMEM((8 * share, cols), BF16),
+            pltpu.VMEM((HD, HD), F32),
+            pltpu.VMEM((16, HD), F32),
         ]
         + sems(2 * TO_TEAM + 2 + GATHER_TEAM + 3 * GATHER_GROUPS // 2 + 16, 9),
         compiler_params=params(1),
         name="start",
-    )(*kinds, gate, up, small, tokens, grad_out)
+    )(*kinds, gate, up, gain_a, gain_f, conv, w_beta, starts, tokens, grad_out)
 
 
 def lanes(at):
@@ -1310,13 +1352,13 @@
     (marks, gains, d_gain_f, x_rows, hidden, d_hidden, ffn_sum), refs = refs[:7], refs[7:]
     (whole, w_out, mixed, normed, branch, part_o, d_down), refs = refs[:7], refs[7:]
     given, refs = refs[:10], refs[10:]
-    (output, d_tokens, got_heads, got_rest, down_sum), refs = refs[:5], refs[5:]
+    (output, d_tokens, got_heads, got_rest, got_ffn, down_sum), refs = refs[:6], refs[6:]
     bufs, refs = refs[:10], refs[10:]
     (w_buf, wo_buf, mixed_buf, normed_buf, rows_buf, do, d_out, d_ext, d_conv), refs = refs[:9], refs[9:]
     (d_head_a, d_head_b, d_small, turned, trade, out_rows, d_rows), refs = refs[:7], refs[7:]
-    (sum_a, sum_b, sum_s, sum_o, packs_heads, packs_rest), refs = refs[:6], refs[6:]
+    (sum_a, sum_b, sum_s, sum_o, packs_heads, packs_rest, packs_ffn), refs = refs[:7], refs[7:]
     own, refs = refs[:7], refs[7:]
-    scratch = [refs[6 * n : 6 * n + 6] for n in range(7)]
+    scratch = [refs[6 * n : 6 * n + 6] for n in range(8)]
     net = Net(*refs[-3:])
     p = net.place
     qkvp, raw, vec, *saved = bufs
@@ -1341,7 +1383,17 @@
     jobs = Jobs(
         output_rows(), out_grad(), scatter_groups(net, d_down, down_sum, cuts[0], *scratch[2])
     )
+    eight, padded, _ = packs_heads.shape
+    spread = thin_rows(ffn_sum.shape[0] // eight, padded).T
+
+    def pack(part, packs, at):
+        wide = mm(spread, part[...]).astype(BF16)
+        packs[:, :, at : at + part.shape[1]] = wide.reshape(eight, padded, part.shape[1])
+
     jobs.step(0)
+    pack(ffn_sum, packs_ffn, 0)
+    early = all_to_team(net, packs_ffn, got_ffn)
+    next(early)
     for copy in first:
         copy.wait()
     third = [net.load(given[m].at[0], bufs[m].at[0]) for m in range(4, 10)]
@@ -1358,7 +1410,7 @@
     for copy in second:
         copy.wait()
     waits = [third, None, None, None, later, None, None, None]
-    steps = [(0,), (), (), (0,), (2, 2), (), (1,), (1,)]
+    steps = [(0,), (), (), (0,), (2, 2), (), (0, 1), (1,)]
 
     def poke():
         jobs.step(*steps.pop(0))
@@ -1388,27 +1440,39 @@
     next(sums_a)
     next(sums_a)
 
-    sums = TeamSum(net, rows_buf, *scratch[5])
+    pieces = [pl.ds(m * n // 2, n // 2) for m in range(2)]
+    sums = [
+        TeamSum(net, rows_buf.at[:, :, piece], *scratch[5 + m]) for m, piece in enumerate(pieces)
+    ]
     turned[...] = jnp.zeros_like(turned)
 
     def work(d):
         at = p.chip(d)
-        total = 0.0
-        for h in range(two):
-            here = pl.ds(pl.multiple_of((h * 8 + 2 * at) * n, 2 * n), 2 * n)
-            y = mm_nt(d_ext[here, :], w_buf[...])
-            total = total + jnp.sum(y * normed_buf[here, :].astype(F32), axis=0, keepdims=True)
-            rows_buf[h, pl.ds(2 * at, 2)] = y.astype(BF16).reshape(2, n, width)
-        turned[0:1, :] += total
-        sums.ready(d)
+        parts = [
+            d_ext[pl.ds(pl.multiple_of((h * 8 + 2 * at) * n, 2 * n), 2 * n), :] for h in range(two)
+        ]
+        y = mm_nt(jnp.concatenate(parts, axis=0), w_buf[...]).astype(BF16)
+        rows_buf[:, pl.ds(2 * at, 2)] = y.reshape(two, 2, n, width)
+        for s in sums:
+            s.ready(d)
 
     work(2)
     work(1)
-    sums.far()
+    for s in sums:
+        s.far()
     work(3)
-    sums.near()
+    for s in sums:
+        s.near()
     work(0)
-    sums.pair(0)
+    for s in sums:
+        s.pair(0)
+    total = 0.0
+    for h in range(two):
+        for t in range(0, 8, 2):
+            here = slice((h * 8 + t) * n, (h * 8 + t + 2) * n)
+            y = rows_buf[h, t : t + 2].reshape(2 * n, width).astype(F32)
+            total = total + jnp.sum(y * normed_buf[here, :].astype(F32), axis=0, keepdims=True)
+    turned[0:1, :] = total
     head_a, head_b = heads_here()
     turned[0:1, :] = turned[0:1, :] / gains[0:1, :]
     turned[1:2, :] = d_gain_f[...]
@@ -1418,35 +1482,30 @@
         part = slice(k * HD, (k + 1) * HD)
         t = mm_tn(normed_buf[:, part], d_ext[:, HEADS_W:]) + turned[:, part].T
         d_small[part, :] = t.astype(BF16)
-    sums_s = scatter_groups(net, d_small, sum_s, cuts[3], *scratch[6])
+    sums_s = scatter_groups(net, d_small, sum_s, cuts[3], *scratch[7])
     next(sums_s)
+    for s in sums:
+        s.on()
     next(sums_b)
     next(sums_b)
-    sums.on()
-    jobs.step(0, 1, 1)
+    swaps = []
+    for s, piece in zip(sums, pieces):
+        d_x, _ = norm_back(x_rows[:, piece].astype(F32), gains[0:1, :][None], s.result())
+        d_rows[:, piece] = (d_x + d_hidden[:, piece]).astype(BF16)
+        swaps.append(swap_rows(net, ((d_rows.at[:, piece], d_tokens.at[:, piece]),)))
+        next(swaps[-1])
+    next(sums_s)
+    jobs.step(1, 1)
     Jobs(sums_a).drain()
     jobs.drain()
-    eight, padded, _ = packs_heads.shape
-    spread = thin_rows(sum_a.shape[0] // eight, padded).T
-
-    def pack(part, packs, at):
-        wide = mm(spread, part[...]).astype(BF16)
-        packs[:, :, at : at + part.shape[1]] = wide.reshape(eight, padded, part.shape[1])
-
     pack(sum_a, packs_rest, 0)
     pack(sum_o, packs_rest, side)
-    pack(ffn_sum, packs_rest, side + 2 * HD)
     rest = all_to_team(net, packs_rest, got_rest)
     next(rest)
-    next(sums_s)
-    d_x, _ = norm_back(x_rows[...].astype(F32), gains[0:1, :][None], sums.result())
-    d_rows[...] = (d_x + d_hidden[...]).astype(BF16)
-    swaps = swap_rows(net, ((d_rows, d_tokens),))
-    next(swaps)
     Jobs(sums_b, sums_s).drain()
     pack(sum_b, packs_heads, 0)
     pack(sum_s, packs_heads, side)
-    interleave(all_to_team(net, packs_heads, got_heads), swaps, rest)
+    interleave(all_to_team(net, packs_heads, got_heads), *swaps, rest, early)
     net.finish()
 
 
@@ -1460,13 +1519,13 @@
     ffn_w = ffn_sum.shape[1]
     cuts = [(0, width // 2, width), (0, HD, 2 * HD), (0, side // 2, side), (0, HD, HD)]
     rows = SHAPE((two, n, width), BF16)
-    packs = [(8, 16, side + HD), (8, 16, side + 2 * HD + ffn_w)]
+    packs = [(8, 16, side + HD), (8, 16, side + 2 * HD), (8, 16, ffn_w)]
     vmem = pltpu.VMEM
     return pl.pallas_call(
         functools.partial(back_kernel, cuts),
         out_shape=[rows, rows] + [SHAPE(a, BF16) for a in packs] + [SHAPE((down, width), F32)],
         in_specs=[VMEM] * 7 + [ANY] * (7 + len(given)),
-        out_specs=[ANY] * 4 + [VMEM],
+        out_specs=[ANY] * 5 + [VMEM],
         scratch_shapes=[vmem((1,) + a.shape[1:] if m > 2 else a.shape, a.dtype) for m, a in enumerate(given)]
         + [
             vmem((width, EXT_W), BF16),
@@ -1497,20 +1556,20 @@
         + scatter_groups_scratch(down, cuts[0])
         + scatter_groups_scratch(r, cuts[2])
         + scatter_groups_scratch(r, cuts[2])
-        + scatter_team_scratch(n, width)
+        + scatter_team_scratch(n // 2, width) * 2
         + scatter_groups_scratch(r, cuts[3])
         + sems(
-            TRADE_BACK + 2 * SCATTER_TEAM + 4 * SCATTER_GROUPS_FLAT + 2 * SCATTER_GROUPS_FLAT + 2 + 2 * TO_TEAM,
-            3 + 3 + 9 + 8 + 4 + SCATTER_TEAM_LOADS + 6 * SCATTER_GROUPS_FLAT_LOADS + 2 + 2,
+            TRADE_BACK + 3 * SCATTER_TEAM + 6 * SCATTER_GROUPS_FLAT + 3 + 3 * TO_TEAM,
+            3 + 3 + 9 + 8 + 4 + SCATTER_TEAM_LOADS + 6 * SCATTER_GROUPS_FLAT_LOADS + 3 + 3,
         ),
         compiler_params=params(5),
         name="back",
     )(*values, *arrays, *given)
 
 
-def unpack_kernel(heads, rest, rows_in, tokens_in, down_in, *outs):
-    kinds, gate, up, small, rows, tokens, down = outs[:5], outs[5], outs[6], outs[7], outs[8], outs[9], outs[10]
-    share = small.shape[0]
+def unpack_kernel(heads, rest, ffn_in, rows_in, tokens_in, down_in, *outs):
+    kinds, (gate, up, gain_a, gain_f, conv, beta, rows, tokens, down) = outs[:5], outs[5:]
+    share = beta.shape[0]
     side = 4 * HD
     for n, out in enumerate(kinds):
         for x in range(4):
@@ -1525,13 +1584,17 @@
     total = heads[0, :, side : side + SMALL_W].astype(F32)
     for t in range(1, 8):
         total = total + heads[t, :, side : side + SMALL_W].astype(F32)
-    small[...] = total[:share]
+    turned = jnp.concatenate([total] * (HD // total.shape[0]), axis=0).T
+    gain_a[...] = turned[0:1, :share]
+    gain_f[...] = turned[1:2, :share]
+    conv[...] = turned[CONV_AT : CONV_AT + TAPS, :share]
+    beta[...] = pltpu.roll(total, HD - BETA_AT, 1)[:share, : beta.shape[1]]
     for n, out in enumerate((gate, up)):
         for tile in range(32):
             e = tile // 2
-            col = side + 2 * HD + n * 4 * HD + (e // 4) * HD
+            col = n * 4 * HD + (e // 4) * HD
             parts = [
-                (rest[t, :, col : col + HD].astype(F32), e % 4)
+                (ffn_in[t, :, col : col + HD].astype(F32), e % 4)
                 for t in range(4 * (tile % 2), 4 * (tile % 2) + 4)
             ]
             out[:, tile * HD : (tile + 1) * HD] = shift_pieces(parts)[:share]
@@ -1540,20 +1603,21 @@
     down[...] = down_in[...]
 
 
-def unpack(heads, rest, rows, tokens, down, share, ff):
+def unpack(heads, rest, ffn_sum, rows, tokens, down, share, ff):
     two, n, width = rows.shape
     return pl.pallas_call(
         unpack_kernel,
         out_shape=[SHAPE((share, width), F32)] * 5
         + [SHAPE((share, ff), F32)] * 2
-        + [SHAPE((share, HD), F32)]
+        + [SHAPE((1, share), F32)] * 2
+        + [SHAPE((TAPS, share), F32), SHAPE((share, 12), F32)]
         + [SHAPE(rows.shape, BF16)] * 2
         + [SHAPE(down.shape, F32)],
-        in_specs=[VMEM] * 5,
-        out_specs=[VMEM] * 11,
+        in_specs=[VMEM] * 6,
+        out_specs=[VMEM] * 14,
         compiler_params=pltpu.CompilerParams(vmem_limit_bytes=VM),
         name="unpack",
-    )(heads, rest, rows, tokens, down)
+    )(heads, rest, ffn_sum, rows, tokens, down)
 
 
 def per_device(
@@ -1573,46 +1637,43 @@
     w_down,
     grad_out,
 ):
-    zh = lax.axis_index("zh")
     width = tokens.shape[2]
     share = w_query.shape[0]
-    small = jnp.concatenate([gain_attn[:, None], gain_ffn[:, None], conv_path.T, w_beta], axis=1)
-    small = jnp.pad(small, ((0, 0), (0, SMALL_W - small.shape[1])))
-    x_rows, g_rows, x_all, whole, own_ffn = start(
-        (w_query, w_key, w_value, w_path, w_out), w_gate, w_up, small, tokens, grad_out
+    x_rows, g_rows, x_all, whole, own_ffn, drow, marks = start(
+        (w_query, w_key, w_value, w_path, w_out),
+        w_gate,
+        w_up,
+        gain_attn[None],
+        gain_ffn[None],
+        conv_path,
+        w_beta,
+        doc_start,
+        tokens,
+        grad_out,
     )
-    doc_rows = jnp.cumsum(doc_start, axis=1)
-    docs = jnp.where(zh == 0, doc_rows[0], doc_rows[1]).astype(F32)
-    marks = [docs]
-    for tap in range(1, TAPS):
-        same = docs[: SEQ - tap] == docs[tap:]
-        marks.append(jnp.concatenate([jnp.zeros((tap,), F32), same.astype(F32)]))
-    drow = jnp.stack(marks + marks)
-    marks = drow.T
-
     normed, qkvp, raw, vec, mixed, gains, *saved, w_ffn, g_all, w_out_t, part = attn_fwd(
         x_all.reshape(SEQ, width), whole, marks, drow, own_ffn, g_rows
     )
     hidden, d_hidden, d_gain_f, branch_all, out_part, ffn_sum, d_down = ffn(
         part, x_rows, g_rows, gains, w_down, w_ffn, g_all
     )
-    output, d_tokens, heads_back, rest_back, d_down = back(
+    output, d_tokens, heads_back, rest_back, ffn_back, d_down = back(
         (marks, gains, d_gain_f, x_rows, hidden, d_hidden, ffn_sum),
         (whole, w_out_t, mixed, normed, branch_all, out_part, d_down),
         (qkvp, raw, vec, *saved),
     )
-    *kinds, d_gate_w, d_up_w, small, output, d_tokens, d_down = unpack(
-        heads_back, rest_back, output, d_tokens, d_down, share, w_gate.shape[1]
+    *kinds, d_gate_w, d_up_w, d_gain_a, d_gain_f, d_conv, d_beta_w, output, d_tokens, d_down = unpack(
+        heads_back, rest_back, ffn_back, output, d_tokens, d_down, share, w_gate.shape[1]
     )
     return (
         output,
         d_tokens,
-        small[:, 0],
+        d_gain_a[0],
         *kinds[:4],
-        small[:, 2:6].T,
-        small[:, 6:18],
+        d_conv,
+        d_beta_w,
         kinds[4],
-        small[:, 1],
+        d_gain_f[0],
         d_gate_w,
         d_up_w,
         d_down,

time: 258 us -> 246 us (0.953)
  local copies, waits for them, and re-layouts: 8.52 us -> 0 us
  other arithmetic: 2.66 us -> 0 us
    slice x3 -> x0, local copies, waits for them, and re-layouts: 3.05 us -> none  [the longest x1 1.47 us: per_device(): small[:, 1]]
where the time goes in v1:
time: 246 us; the launch traced here: 242 us
  Pallas kernels  241 us (98%)
    pallas_call x1, Pallas kernels, ffn(): pl.pallas_call(functools.partial(ffn_kernel, cuts), out_shape=[SHAPE((two...  78.6 us
    pallas_call x1, Pallas kernels, back(): pl.pallas_call(functools.partial(back_kernel, cuts), out_shape=[rows, row...  75 us
    pallas_call x1, Pallas kernels, start(): pl.pallas_call(start_kernel, out_shape=[rows, rows, SHAPE((two, 8, n, wid...  48.8 us
    pallas_call x1, Pallas kernels, attn_fwd(): pl.pallas_call(attn_fwd_kernel, out_shape=[SHAPE(*a) for a in kept] + [SH...  35.7 us

profile of v1, /device:TPU:1, one launch (start us, length us, event | category | flops | bytes accessed | tf_op | source)
XLA Modules:
  0.0 242.2 jit_solution(8222801386155373472)
XLA Ops:
  0.7 48.8 %start.1 = (bf16[2,64,1536]{2,1,0:T(8,128)(2,1)}, bf16[2,64,1536]{2,1,0:T(8,128)(2,1)}, bf16[2,8,64,1536]{3,2,1,0:T(8,128)(2,1)}, bf16[1536,1408]{1,0:T(8,128)(2...) custom-call(bf16[12,1536]{1,0:T(8,128)(2,1)} %wq.1, bf16[12,1536]{1,0:T(8,128)(2,1)} %wk.1, ...), custom_call_target="tpu_custom_call" | custom-call | tf_op jit(solution)/shard_map/start/pallas_call | solution.py:904
  49.5 35.7 %attn_fwd.1 = (bf16[1024,1536]{1,0:T(8,128)(2,1)}, bf16[1024,1024]{1,0:T(8,128)(2,1)}, f32[1024,128]{1,0:T(8,128)}, bf16[1024,256]{1,0:T(8,128)(2,1)}, bf16[1024...) custom-call(bf16[1024,1536]{1,0:T(8,128)(2,1)} %bitcast.5, ...), custom_call_target="tpu_custom_call" | custom-call | tf_op jit(solution)/shard_map/attn_fwd/pallas_call | solution.py:1009
  85.1 78.6 %ffn.1 = (f32[2,64,1536]{2,1,0:T(8,128)}, f32[2,64,1536]{2,1,0:T(8,128)}, f32[1,1536]{1,0:T(1,128)}, bf16[2,8,64,1536]{3,2,1,0:T(8,128)(2,1)}, bf16[2,8,64,1536]...) custom-call(bf16[2,8,64,1536]{3,2,1,0:T(8,128)(2,1)} %get-tuple-element.72.refs_0_, ...), custom_call_target="tpu_custom_call" | custom-call | tf_op jit(solution)/shard_map/ffn/pallas_call | solution.py:1257
  163.8 75.0 %back.1 = (bf16[2,64,1536]{2,1,0:T(8,128)(2,1)}, bf16[2,64,1536]{2,1,0:T(8,128)(2,1)}, bf16[8,16,640]{2,1,0:T(8,128)(2,1)}, bf16[8,16,768]{2,1,0:T(8,128)(2,1)},...) custom-call(f32[1024,8]{1,0:T(8,128)} %get-tuple-element.65.marks.refs_0_, ...), custom_call_target="tpu_custom_call" | custom-call | tf_op jit(solution)/shard_map/back/pallas_call | solution.py:1524
  238.8 2.9 %unpack.1 = (f32[12,1536]{1,0:T(8,128)}, f32[12,1536]{1,0:T(8,128)}, f32[12,1536]{1,0:T(8,128)}, f32[12,1536]{1,0:T(8,128)}, f32[12,1536]{1,0:T(8,128)}, /*index...) custom-call(bf16[8,16,640]{2,1,0:T(8,128)(2,1)} %get-tuple-element.9, ...), custom_call_target="tpu_custom_call" | custom-call | tf_op jit(solution)/shard_map/unpack/pallas_call | solution.py:1608

commit v2 on v1

--- a/solution.py
+++ b/solution.py
@@ -860,9 +860,8 @@
     meet(team_all(p) + group_peers(p))
     trades = [all_to_team(net, packs.at[:, :, part], got.at[:, :, part]) for part in (first, second)]
     swaps = [swap_rows(net, (pair,)) for pair in ((tokens, x_rows), (grad_out, g_rows))]
-    for n in range(2):
-        next(trades[n])
-        next(swaps[n])
+    next(trades[0])
+    next(swaps[0])
     pick = thin_rows(share, packs.shape[1])
 
     def thin(part):
@@ -886,10 +885,13 @@
     interleave(swaps[0])
     x_team = gather_team(net, x_rows, x_all)
     next(x_team)
+    next(trades[1])
+    next(swaps[1])
     for _ in range(3):
         next(heads)
     next(x_team)
     interleave(trades[1])
+    net.settle()
     thin(second)
     net.keep(own.at[:, second], own_ffn)
     interleave(x_team, heads, swaps[1])
@@ -1127,7 +1129,7 @@
     (part, x_rows, g_rows, gain, own_down, w_ffn, g_all), refs = refs[:7], refs[7:]
     (hidden, d_hidden, d_gain, branch_all, out_part, ffn_sum, down_out), refs = refs[:7], refs[7:]
     (w_in, w_down, g_buf, nf_all, normed, act, d_in, back, branch, d_ffn, d_down, out_buf), refs = refs[:12], refs[12:]
-    scratch = [refs[6 * n : 6 * n + 6] for n in range(5)]
+    scratch = [refs[6 * n : 6 * n + 6] for n in range(6)]
     net = Net(*refs[-3:])
     p = net.place
     loads = [net.load(w_ffn, w_in), net.load(g_all, g_buf)]
@@ -1209,14 +1211,17 @@
         s.pair(0)
     rows = two * 8 * n
     step = width // 4
-    for k in range(4):
-        cols = slice(k * step, (k + 1) * step)
-        left = nf_all[:, :, :, cols].reshape(rows, step)
-        d_ffn[cols, :] = mm_tn(left, d_in[...].reshape(rows, 2 * half)).astype(BF16)
-        if k in (1, 2):
-            sums[k - 1].on()
-    group = scatter_groups(net, d_ffn, ffn_sum, cuts, *scratch[4])
-    next(group)
+    groups = []
+    for side in range(2):
+        right = d_in[:, :, :, side * half : (side + 1) * half].reshape(rows, half)
+        for k in range(4):
+            cols = slice(k * step, (k + 1) * step)
+            left = nf_all[:, :, :, cols].reshape(rows, step)
+            d_ffn[side, cols, :] = mm_tn(left, right).astype(BF16)
+        place = ffn_sum.at[:, pl.ds(side * half, half)]
+        groups.append(scatter_groups(net, d_ffn.at[side], place, cuts, *scratch[4 + side]))
+        next(groups[-1])
+        sums[side].on()
     d_gain[...] = jnp.zeros_like(d_gain)
     teams = []
     for s, piece in zip(sums, pieces):
@@ -1240,9 +1245,10 @@
     net.keep(out_buf, out_part)
     for team in teams:
         next(team)
-    next(group)
-    next(group)
-    jobs = Jobs(*teams, group)
+    for _ in range(2):
+        for group in groups:
+            next(group)
+    jobs = Jobs(*teams, *groups)
     jobs.drain()
     net.finish()
 
@@ -1253,7 +1259,7 @@
     half, rows = cols // 2, own_down.shape[0]
     every = (two, 8, n, width)
     share = width // 16
-    cuts = (0, half, cols)
+    cuts = (0, half // 2, half)
     return pl.pallas_call(
         functools.partial(ffn_kernel, cuts),
         out_shape=[
@@ -1277,15 +1283,15 @@
             pltpu.VMEM((two, 8, n, cols), BF16),
             pltpu.VMEM(every, BF16),
             pltpu.VMEM((two, n, width), BF16),
-            pltpu.VMEM((width, cols), BF16),
+            pltpu.VMEM((2, width, half), BF16),
             pltpu.VMEM((half, width), BF16),
             pltpu.VMEM(every, BF16),
         ]
         + scatter_team_scratch(n // 2, width) * 4
-        + scatter_groups_scratch(share, cuts)
+        + scatter_groups_scratch(share, cuts) * 2
         + sems(
-            4 * SCATTER_TEAM + 4 * GATHER_TEAM + GATHER_GROUPS + SCATTER_GROUPS_FLAT,
-            2 + 2 * SCATTER_TEAM_LOADS + 2 + 2 + 2 + 2 + SCATTER_GROUPS_FLAT_LOADS,
+            4 * SCATTER_TEAM + 4 * GATHER_TEAM + GATHER_GROUPS + 2 * SCATTER_GROUPS_FLAT,
+            2 + 2 * SCATTER_TEAM_LOADS + 2 + 2 + 2 + 2 + 2 * SCATTER_GROUPS_FLAT_LOADS,
         ),
         compiler_params=params(3),
         name="ffn",
@@ -1404,13 +1410,13 @@
     do[:, :HD] = d_mixed[:, :HD]
     do[:, HD:] = jnp.where(p.c == 0, d_mixed[:, HD:], 0.0)
     d_out[...] = mm_tn(mixed_buf[...], branch_rows).astype(BF16)
-    jobs.step(1, 2)
+    jobs.step(2)
     fourth = [net.load(normed, normed_buf)]
     later = []
     for copy in second:
         copy.wait()
     waits = [third, None, None, None, later, None, None, None]
-    steps = [(0,), (), (), (0,), (2, 2), (), (0, 1), (1,)]
+    steps = [(0,), (), (), (0, 1), (2, 2), (), (0,), (1, 1)]
 
     def poke():
         jobs.step(*steps.pop(0))

time: 246 us -> 236 us (0.959)
  Pallas kernels: 241 us -> 232 us
    pallas_call x1, Pallas kernels: 78.6 us -> 74.3 us  [ffn(): pl.pallas_call(functools.partial(ffn_kernel, cuts), out_shape=[SHAPE((two...]
    pallas_call x1, Pallas kernels: 48.8 us -> 45.1 us  [start(): pl.pallas_call(start_kernel, out_shape=[rows, rows, SHAPE((two, 8, n, wid...]
where the time goes in v2:
time: 236 us; the launch traced here: 233 us
  Pallas kernels  232 us (98%)
    pallas_call x1, Pallas kernels, ffn(): pl.pallas_call(functools.partial(ffn_kernel, cuts), out_shape=[SHAPE((two...  74.3 us
    pallas_call x1, Pallas kernels, back(): pl.pallas_call(functools.partial(back_kernel, cuts), out_shape=[rows, row...  72.9 us
    pallas_call x1, Pallas kernels, start(): pl.pallas_call(start_kernel, out_shape=[rows, rows, SHAPE((two, 8, n, wid...  45.1 us
    pallas_call x1, Pallas kernels, attn_fwd(): pl.pallas_call(attn_fwd_kernel, out_shape=[SHAPE(*a) for a in kept] + [SH...  36.4 us

profile of v2, /device:TPU:1, one launch (start us, length us, event | category | flops | bytes accessed | tf_op | source)
XLA Modules:
  0.0 232.8 jit_solution(3607378761297568249)
XLA Ops:
  0.7 45.1 %start.1 = (bf16[2,64,1536]{2,1,0:T(8,128)(2,1)}, bf16[2,64,1536]{2,1,0:T(8,128)(2,1)}, bf16[2,8,64,1536]{3,2,1,0:T(8,128)(2,1)}, bf16[1536,1408]{1,0:T(8,128)(2...) custom-call(bf16[12,1536]{1,0:T(8,128)(2,1)} %wq.1, bf16[12,1536]{1,0:T(8,128)(2,1)} %wk.1, ...), custom_call_target="tpu_custom_call" | custom-call | tf_op jit(solution)/shard_map/start/pallas_call | solution.py:906
  45.8 36.4 %attn_fwd.1 = (bf16[1024,1536]{1,0:T(8,128)(2,1)}, bf16[1024,1024]{1,0:T(8,128)(2,1)}, f32[1024,128]{1,0:T(8,128)}, bf16[1024,256]{1,0:T(8,128)(2,1)}, bf16[1024...) custom-call(bf16[1024,1536]{1,0:T(8,128)(2,1)} %bitcast.5, ...), custom_call_target="tpu_custom_call" | custom-call | tf_op jit(solution)/shard_map/attn_fwd/pallas_call | solution.py:1011
  82.2 74.3 %ffn.1 = (f32[2,64,1536]{2,1,0:T(8,128)}, f32[2,64,1536]{2,1,0:T(8,128)}, f32[1,1536]{1,0:T(1,128)}, bf16[2,8,64,1536]{3,2,1,0:T(8,128)(2,1)}, bf16[2,8,64,1536]...) custom-call(bf16[2,8,64,1536]{3,2,1,0:T(8,128)(2,1)} %get-tuple-element.72.refs_0_, ...), custom_call_target="tpu_custom_call" | custom-call | tf_op jit(solution)/shard_map/ffn/pallas_call | solution.py:1263
  156.5 72.9 %back.1 = (bf16[2,64,1536]{2,1,0:T(8,128)(2,1)}, bf16[2,64,1536]{2,1,0:T(8,128)(2,1)}, bf16[8,16,640]{2,1,0:T(8,128)(2,1)}, bf16[8,16,768]{2,1,0:T(8,128)(2,1)},...) custom-call(f32[1024,8]{1,0:T(8,128)} %get-tuple-element.65.marks.refs_0_, ...), custom_call_target="tpu_custom_call" | custom-call | tf_op jit(solution)/shard_map/back/pallas_call | solution.py:1530
  229.4 2.9 %unpack.1 = (f32[12,1536]{1,0:T(8,128)}, f32[12,1536]{1,0:T(8,128)}, f32[12,1536]{1,0:T(8,128)}, f32[12,1536]{1,0:T(8,128)}, f32[12,1536]{1,0:T(8,128)}, /*index...) custom-call(bf16[8,16,640]{2,1,0:T(8,128)(2,1)} %get-tuple-element.9, ...), custom_call_target="tpu_custom_call" | custom-call | tf_op jit(solution)/shard_map/unpack/pallas_call | solution.py:1614
